TPU v7x, 32 devices: a whole 2x2x4 slice. The times are simulated.
32 devices in a mesh: groups: 2 (over x), gx: 4 (over y, core), gy: 4 (over z).
Axes of the slice: x: 2, y: 2, z: 4, core: 2. Of those that a mesh axis runs over, the one named last changes fastest.
Arguments:
- cell_start: float32 [2, 8, 64, 1024], P(None, None, ('groups', 'gx'), 'gy'), parts along dimension 2, may hold values from -6 to 6
- diffusivity: float32 [2, 8, 64, 1024], P(None, None, ('groups', 'gx'), 'gy'), parts along dimension 2, may hold values from 0.01 to 0.07
- host_cell: int32 [262144], P(('groups', 'gx', 'gy')), parts along dimension 0, may hold values from 0 to 16383
- disp_start: float32 [6, 262144], P(None, ('groups', 'gx', 'gy')), parts along dimension 1, may hold values from -3 to 3
- vel_start: float32 [6, 262144], P(None, ('groups', 'gx', 'gy')), parts along dimension 1, may hold values from -3 to 3
- inertia: float32 [2, 262144], P(None, ('groups', 'gx', 'gy')), parts along dimension 1, may hold values from 1 to 4
- facet_own: int32 [524288], P(('groups', 'gx', 'gy')), parts along dimension 0, may hold values from 0 to 8191
- facet_other: int32 [524288], P(('groups', 'gx', 'gy')), parts along dimension 0, may hold values from 0 to 24575
- facet_arms: float32 [6, 524288], P(None, ('groups', 'gx', 'gy')), parts along dimension 1, may hold values from -3 to 3
- facet_frame: float32 [9, 524288], P(None, ('groups', 'gx', 'gy')), parts along dimension 1, may hold values from -3 to 3
- facet_stiffness: float32 [2, 524288], P(None, ('groups', 'gx', 'gy')), parts along dimension 1, may hold values from 0.2 to 1
- facet_eigen: float32 [2, 524288], P(None, ('groups', 'gx', 'gy')), parts along dimension 1, may hold values from 0.2 to 1
- live_blocks: int32 [32], P(('groups', 'gx', 'gy')), parts along dimension 0, may hold values from 1 to 128, as said below
Outputs:
- cell_state: float32 [2, 8, 64, 1024], P(None, None, ('groups', 'gx'), 'gy'), parts along dimension 2
- particle_disp: float32 [6, 262144], P(None, ('groups', 'gx', 'gy')), parts along dimension 1
- particle_vel: float32 [6, 262144], P(None, ('groups', 'gx', 'gy')), parts along dimension 1
There are 2 independent parts, one for each index of `groups`. A program takes and returns all parts, laid end to end along the dimension named above; each array names one. Nothing has to cross between parts.
Inputs may be any that keep to these rules, and one draw needn't show every extreme that they name: `live_blocks`: partitions with thickness index 0 have all 128 blocks live; others at least a quarter of them.
All inputs are finite; a program needn't handle non-finite values.
Results may differ from a plain program's by a relative error of at most 0.0001.
Values sent between devices are 32-bit elements; how exact they have to be, the bound alone decides.
A program may use at most 128 MiB of HBM per device.

v0:
```python
import jax
import jax.numpy as jnp
from jax import lax
from jax.sharding import PartitionSpec as P

couple_rate = 0.1
time_step = 0.2


def padded_2(block, sides, width):
    for axis, dim in sides:
        count = lax.axis_size(axis)
        forward = [(i, i + 1) for i in range(count - 1)]
        backward = [(target, source) for source, target in forward]
        low = lax.ppermute(
            lax.slice_in_dim(block, block.shape[dim] - width, None, axis=dim), axis, forward
        )
        high = lax.ppermute(lax.slice_in_dim(block, 0, width, axis=dim), axis, backward)
        block = jnp.concatenate([low, block, high], axis=dim)
    return block


def advance_plan(extended, rates):
    padded = jnp.pad(extended, ((0, 0), (1, 1), (0, 0), (0, 0)))
    center = padded[:, 1:-1, 1:-1, 1:-1]
    laplace = padded[:, 2:, 1:-1, 1:-1] + padded[:, :-2, 1:-1, 1:-1]
    laplace = laplace + padded[:, 1:-1, 2:, 1:-1] + padded[:, 1:-1, :-2, 1:-1]
    laplace = laplace + padded[:, 1:-1, 1:-1, 2:] + padded[:, 1:-1, 1:-1, :-2] - 6.0 * center
    return center + rates * laplace + couple_rate * (center[::-1] - center)


def cross_rows(left, right):
    return jnp.stack(
        [
            left[1] * right[2] - left[2] * right[1],
            left[2] * right[0] - left[0] * right[2],
            left[0] * right[1] - left[1] * right[0],
        ]
    )


def facet_load(own_rows, window, own_idx, other_idx, arms, frame, stiff, eigen, weight_mask):
    side_a = own_rows[:, own_idx]
    side_b = window[:, other_idx]
    arm_a = arms[0:3]
    arm_b = arms[3:6]
    relative = (
        side_b[0:3] + cross_rows(side_b[3:6], arm_b) - side_a[0:3] - cross_rows(side_a[3:6], arm_a)
    )
    strain = [
        frame[3 * k] * relative[0] + frame[3 * k + 1] * relative[1] + frame[3 * k + 2] * relative[2]
        for k in range(3)
    ]
    eigen_strain = 0.5 * (eigen[0] * (side_a[7] + side_b[7]) + eigen[1] * (side_a[6] + side_b[6]))
    stress = [stiff[0] * (strain[0] - eigen_strain), stiff[1] * strain[1], stiff[1] * strain[2]]
    force = jnp.stack(
        [
            stress[0] * frame[m] + stress[1] * frame[3 + m] + stress[2] * frame[6 + m]
            for m in range(3)
        ]
    )
    moment = cross_rows(arm_a, force)
    terms = jnp.concatenate([force, moment], axis=0) * weight_mask
    segments = own_rows.shape[1]
    return jax.vmap(lambda row: jax.ops.segment_sum(row, own_idx, num_segments=segments))(terms)


def body(
    cell_start,
    diffusivity,
    host_cell,
    disp_start,
    vel_start,
    inertia,
    facet_own,
    facet_other,
    facet_arms,
    facet_frame,
    facet_stiffness,
    facet_eigen,
    live_blocks,
):
    state = cell_start
    for substep in range(3):
        extended = padded_2(state, (("gx", 2), ("gy", 3)), 1)
        state = advance_plan(extended, diffusivity)
    layers = state.shape[1]
    slab_rows = layers // lax.axis_size("gy")
    gathered = lax.all_gather(state, "gy", axis=3, tiled=True)
    slab = lax.dynamic_slice_in_dim(gathered, lax.axis_index("gy") * slab_rows, slab_rows, 1)
    fields = slab.reshape(2, -1)[:, host_cell]
    part_count = disp_start.shape[1]
    facet_count = facet_own.shape[0]
    masses = jnp.repeat(inertia, 3, axis=0)
    live = live_blocks[0]
    block_ids = jnp.arange(facet_count, dtype=jnp.int32) // 128
    weight_mask = (block_ids < live).astype(jnp.float32)[None, :]
    disp = disp_start
    vel = vel_start
    for substep in range(2):
        own_rows = jnp.concatenate([disp, fields], axis=0)
        window = padded_2(own_rows, (("gx", 1),), part_count)
        loads = facet_load(
            own_rows,
            window,
            facet_own,
            facet_other,
            facet_arms,
            facet_frame,
            facet_stiffness,
            facet_eigen,
            weight_mask,
        )
        vel = vel + time_step * loads / masses
        disp = disp + time_step * vel
    return (state, disp, vel)


def solution(mesh):
    return jax.shard_map(
        body,
        mesh=mesh,
        in_specs=(
            P(None, None, ("groups", "gx"), "gy"),
            P(None, None, ("groups", "gx"), "gy"),
            P(("groups", "gx", "gy")),
            P(None, ("groups", "gx", "gy")),
            P(None, ("groups", "gx", "gy")),
            P(None, ("groups", "gx", "gy")),
            P(("groups", "gx", "gy")),
            P(("groups", "gx", "gy")),
            P(None, ("groups", "gx", "gy")),
            P(None, ("groups", "gx", "gy")),
            P(None, ("groups", "gx", "gy")),
            P(None, ("groups", "gx", "gy")),
            P(("groups", "gx", "gy")),
        ),
        out_specs=(
            P(None, None, ("groups", "gx"), "gy"),
            P(None, ("groups", "gx", "gy")),
            P(None, ("groups", "gx", "gy")),
        ),
        check_vma=False,
    )
```

profile of v0, /device:TPU:1, one launch (start us, length us, event | category | flops | bytes accessed | tf_op | source)
XLA Modules:
  0.0 635.5 jit_solution(16385190353120798675)
XLA Ops:
  0.7 1.0 fusion.53
  1.7 4.5 collective-permute-start
  6.2 1.9 collective-permute-start.1
  8.2 3.1 collective-permute-done.1
  11.3 1.0 pad_maximum_fusion.3
  12.4 3.2 collective-permute-start.2
  15.6 1.3 collective-permute-start.3
  16.9 0.9 fusion.37
  17.8 3.7 collective-permute-done.3
  21.5 1.2 select_maximum_fusion.8
  22.7 1.6 fusion.8
  24.3 3.2 collective-permute-start.4
  27.5 1.9 collective-permute-start.5
  30.3 2.2 collective-permute-done.5
  32.7 3.2 collective-permute-start.6
  36.0 1.3 collective-permute-start.7
  38.7 3.2 collective-permute-done.7
  42.2 1.2 fusion.10
  43.4 3.2 collective-permute-start.8
  46.6 1.9 collective-permute-start.9
  48.6 3.1 collective-permute-done.9
  51.8 3.2 collective-permute-start.10
  55.0 1.3 collective-permute-start.11
  56.3 3.5 copy.540
  60.0 0.9 collective-permute-done.11
  61.5 14.0 %all_gather.3 = f32[2,8,8,1024]{3,2,1,0:T(8,128)S(1)} all-gather(f32[2,8,8,256]{3,2,1,0:T(8,128)S(1)} %fusion.12), channel_id=1, replica_groups=mesh['groups'=2,'gx'=4,'gy'=4] {'gy'}, dimensions={3}, use_global_device_ids=true | all-gather | bytes 655360 | tf_op jit(solution)/shard_map/all_gather | solution.py:89
  75.5 4.6 copy.538
  80.1 31.1 %gather_fusion = f32[8192,2]{1,0:T(8,128)} fusion(f32[2,16384]{0,1:T(8,128)} %bitcast.12, s32[8192]{0:T(1024)S(1)} %fusion.47), kind=kCustom, calls=%fused_computation | custom fusion | bytes 163840 | tf_op jit(solution)/shard_map/gather | solution.py:91
  111.3 2.8 copy.539
  114.1 2.6 copy.541
  116.8 6.6 %pad_maximum_fusion.1 = f32[8,8192]{0,1:T(8,128)} fusion(f32[2,8192]{0,1:T(8,128)} %copy.541, f32[6,8192]{0,1:T(8,128)} %copy.540), kind=kLoop, calls=%fused_computation.8 | loop fusion | flops 65536 | bytes 524288 | tf_op jit(solution)/shard_map/concatenate | solution.py:101
  123.4 2.8 copy.542
  126.2 3.9 collective-permute-start.12
  130.2 2.1 collective-permute-start.13
  132.3 56.7 %gather_fusion.2 = f32[16384,8]{1,0:T(8,128)} fusion(f32[8,8192]{0,1:T(8,128)} %pad_maximum_fusion.1, s32[16384]{0:T(1024)S(1)} %fusion.38), kind=kCustom, calls=%fused_computation.2 | custom fusion | bytes 1114112 | tf_op jit(solution)/shard_map/gather | solution.py:43
  189.0 5.5 copy.547
  194.9 2.7 copy.544
  197.6 2.7 copy.545
  200.2 15.2 %pad_maximum_fusion = f32[8,24576]{0,1:T(8,128)} fusion(f32[8,8192]{0,1:T(8,128)} %copy.545, f32[2,8192]{0,1:T(8,128)} %copy.541, f32[6,8192]{0,1:T(8,128)} %copy.540, f32[8,8192]{0,1:T(8,128)} %copy.544), kind=kLoop, calls=%fused_computation.7 | loop fusion | flops 589824 | bytes 1572864 | tf_op jit(solution)/shard_map/concatenate | solution.py:19
  215.4 59.1 %gather_fusion.1 = f32[16384,8]{1,0:T(8,128)} fusion(f32[8,24576]{0,1:T(8,128)} %pad_maximum_fusion, s32[16384]{0:T(1024)S(1)} %fusion.37), kind=kCustom, calls=%fused_computation.1 | custom fusion | bytes 1114112 | tf_op jit(solution)/shard_map/gather | solution.py:44
  274.6 5.5 copy.546
  280.9 2.9 multiply_subtract_fusion.9
  284.2 1.4 concatenate.92
  285.7 5.4 copy.548
  291.1 89.8 %scatter_custom_fusion = f32[6,8192]{0,1:T(8,128)} fusion(s32[16384]{0:T(1024)} %param.19, f32[16384,6]{1,0:T(8,128)} %copy.548, f32[]{:T(128)} %constant.16.clone.1), kind=kCustom, calls=%fused_computation.11 | custom fusion | flops 98304 | bytes 197120 | tf_op jit(solution)/shard_map/vmap()/scatter-add | solution.py:65
  380.9 2.8 copy.549
  383.9 3.6 collective-permute-start.14
  387.6 1.9 collective-permute-start.15
  389.5 2.7 copy.552
  392.2 56.7 %gather_fusion.4 = f32[16384,8]{1,0:T(8,128)} fusion(f32[8,8192]{0,1:T(8,128)} %copy.552, s32[16384]{0:T(1024)S(1)} %copy-done.9), kind=kCustom, calls=%fused_computation.4 | custom fusion | bytes 1114112 | tf_op jit(solution)/shard_map/gather | solution.py:43
  448.8 5.5 copy.553
  454.4 1.1 multiply_subtract_fusion.5
  456.2 1.1 pad_maximum_fusion.2
  457.3 7.3 %copy.550 = f32[8,24576]{0,1:T(8,128)} copy(f32[8,24576]{1,0:T(8,128)S(1)} %pad_maximum_fusion.2) | data formatting | bytes 1572864 | tf_op jit(solution)/shard_map/concatenate | solution.py:19
  464.7 59.1 %gather_fusion.3 = f32[16384,8]{1,0:T(8,128)} fusion(f32[8,24576]{0,1:T(8,128)} %copy.550, s32[16384]{0:T(1024)S(1)} %fusion.37), kind=kCustom, calls=%fused_computation.3 | custom fusion | bytes 1114112 | tf_op jit(solution)/shard_map/gather | solution.py:44
  523.7 5.6 copy.551
  529.7 1.2 fusion.5
  530.9 2.9 multiply_subtract_fusion
  534.3 1.4 concatenate.95
  535.6 0.9 multiply_bitcast_fusion
  536.6 5.4 copy.554
  541.9 89.8 %scatter_custom_fusion.1 = f32[6,8192]{0,1:T(8,128)} fusion(s32[16384]{0:T(1024)} %param.19, f32[16384,6]{1,0:T(8,128)} %copy.554, f32[]{:T(128)} %constant.16.clone.1), kind=kCustom, calls=%fused_computation.9 | custom fusion | flops 98304 | bytes 197120 | tf_op jit(solution)/shard_map/vmap()/scatter-add | solution.py:65
  631.7 2.8 copy.555
  634.6 0.9 multiply_add_fusion
  (69 shorter events, 6.4 us)
Async XLA Ops:
  0.6 60.6 %copy-start.4 = (f32[2,8,8,256]{3,2,1,0:T(8,128)S(1)}, f32[2,8,8,256]{3,2,1,0:T(8,128)}, u32[]{:S(2)}) copy-start(f32[2,8,8,256]{3,2,1,0:T(8,128)} %param.14) | copy-start | bytes 393220
  0.6 59.2 %copy-start.15 = (f32[2,8192]{1,0:T(2,128)S(1)}, f32[2,8192]{1,0:T(2,128)}, u32[]{:S(2)}) copy-start(f32[2,8192]{1,0:T(2,128)} %param.18) | copy-start | bytes 196612
  1.7 6.5 %collective-permute-start = (f32[2,8,1,256]{3,2,1,0:T(1,128)S(1)}, f32[2,8,1,256]{3,2,1,0:T(1,128)S(1)}, u32[]{:S(2)}, u32[]{:S(2)}) collective-permute-start(f32[2,8,1,256]{3,2,1,0:T(1,128)S(1)} %get-tuple-element.58), channel_id=1, source_target_pairs={{0,4},{4,8},{8,12},{1,5},{5,9},{9,13},{2,6},{6,10},{10,14},{3,7},{... | collective-permute-start | bytes 49160 | tf_op jit(solution)/shard_map/ppermute | solution.py:15
  6.2 5.1 collective-permute-start.1
  12.4 5.4 collective-permute-start.2
  15.6 5.9 collective-permute-start.3
  24.3 6.0 collective-permute-start.4
  27.5 5.1 collective-permute-start.5
  30.3 101.9 %copy-start.8 = (s32[16384]{0:T(1024)}, s32[16384]{0:T(1024)S(1)}, u32[]{:S(2)}) copy-start(s32[16384]{0:T(1024)S(1)} %fusion.38) | copy-start | bytes 196612
  32.7 5.9 collective-permute-start.6
  36.0 5.9 collective-permute-start.7
  43.4 5.2 collective-permute-start.8
  46.6 5.1 collective-permute-start.9
  48.5 237.1 %copy-start.10 = (f32[16384]{0:T(1024)}, f32[16384]{0:T(1024)S(1)}, u32[]{:S(2)}) copy-start(f32[16384]{0:T(1024)S(1)} %fusion.46) | copy-start | bytes 196612
  51.8 8.2 %collective-permute-start.10 = (f32[2,8,10,1]{3,2,1,0:T(8,128)S(1)}, f32[2,8,10,1]{3,2,1,0:T(8,128)S(1)}, u32[]{:S(2)}, u32[]{:S(2)}) collective-permute-start(f32[2,8,10,1]{3,2,1,0:T(8,128)S(1)} %get-tuple-element.49), channel_id=1, source_target_pairs={{0,1},{1,2},{2,3},{4,5},{5,6},{6,7},{8,9},{9,10},{10,11},{12,13},{... | collective-permute-start | bytes 1928 | tf_op jit(solution)/shard_map/ppermute | solution.py:15
  55.0 5.9 collective-permute-start.11
  60.0 323.8 %copy-start.2 = (f32[6,8192]{1,0:T(8,128)}, f32[6,8192]{1,0:T(8,128)S(1)}, u32[]{:S(2)}) copy-start(f32[6,8192]{1,0:T(8,128)S(1)} %reshape.28) | copy-start | bytes 589828
  61.5 55.2 %copy-start.11 = (f32[2,8,8,256]{3,2,1,0:T(8,128)}, f32[2,8,8,256]{3,2,1,0:T(8,128)S(1)}, u32[]{:S(2)}) copy-start(f32[2,8,8,256]{3,2,1,0:T(8,128)S(1)} %fusion.12) | copy-start | bytes 393220
  123.4 71.1 %copy-start = (f32[6,16384]{1,0:T(8,128)S(1)}, f32[6,16384]{1,0:T(8,128)}, u32[]{:S(2)}) copy-start(f32[6,16384]{1,0:T(8,128)} %param.21) | copy-start | bytes 1179652
  126.2 68.6 %collective-permute-start.12 = (f32[8,8192]{1,0:T(8,128)S(1)}, f32[8,8192]{1,0:T(8,128)S(1)}, u32[]{:S(2)}, u32[]{:S(2)}) collective-permute-start(f32[8,8192]{1,0:T(8,128)S(1)} %copy.542), channel_id=1, source_target_pairs={{0,4},{4,8},{8,12},{1,5},{5,9},{9,13},{2,6},{6,10},{10,14},{3,7},{... | collective-permute-start | bytes 786440 | tf_op jit(solution)/shard_map/ppermute | solution.py:15
  130.2 67.4 %collective-permute-start.13 = (f32[8,8192]{1,0:T(8,128)S(1)}, f32[8,8192]{1,0:T(8,128)S(1)}, u32[]{:S(2)}, u32[]{:S(2)}) collective-permute-start(f32[8,8192]{1,0:T(8,128)S(1)} %copy.542), channel_id=1, source_target_pairs={{4,0},{8,4},{12,8},{5,1},{9,5},{13,9},{6,2},{10,6},{14,10},{7,3},{... | collective-permute-start | bytes 786440 | tf_op jit(solution)/shard_map/ppermute | solution.py:18
  215.4 65.4 %copy-start.1 = (f32[9,16384]{1,0:T(8,128)S(1)}, f32[9,16384]{1,0:T(8,128)}, u32[]{:S(2)}) copy-start(f32[9,16384]{1,0:T(8,128)} %param.22) | copy-start | bytes 1769476
  285.7 98.0 %copy-start.5 = (f32[6,8192]{1,0:T(8,128)S(1)}, f32[6,8192]{1,0:T(8,128)}, u32[]{:S(2)}) copy-start(f32[6,8192]{1,0:T(8,128)} %param.16) | copy-start | bytes 589828
  285.7 98.0 %copy-start.6 = (f32[6,8192]{1,0:T(8,128)S(1)}, f32[6,8192]{1,0:T(8,128)}, u32[]{:S(2)}) copy-start(f32[6,8192]{1,0:T(8,128)} %param.17) | copy-start | bytes 589828
  291.1 101.1 %copy-start.9 = (s32[16384]{0:T(1024)S(1)}, s32[16384]{0:T(1024)}, u32[]{:S(2)}) copy-start(s32[16384]{0:T(1024)} %copy-done.8) | copy-start | bytes 196612
  383.9 71.6 %collective-permute-start.14 = (f32[8,8192]{1,0:T(8,128)S(1)}, f32[8,8192]{1,0:T(8,128)S(1)}, u32[]{:S(2)}, u32[]{:S(2)}) collective-permute-start(f32[8,8192]{1,0:T(8,128)S(1)} %pad_maximum_fusion.6), channel_id=1, source_target_pairs={{0,4},{4,8},{8,12},{1,5},{5,9},{9,13},{2,6},{6,10},{10,14},{3,7},{... | collective-permute-start | bytes 786440 | tf_op jit(solution)/shard_map/ppermute | solution.py:15
  387.6 68.7 %collective-permute-start.15 = (f32[8,8192]{1,0:T(8,128)S(1)}, f32[8,8192]{1,0:T(8,128)}, u32[]{:S(2)}, u32[]{:S(2)}) collective-permute-start(f32[8,8192]{1,0:T(8,128)S(1)} %pad_maximum_fusion.6), channel_id=1, source_target_pairs={{4,0},{8,4},{12,8},{5,1},{9,5},{13,9},{6,2},{10,6},{14,10},{7,3},{... | collective-permute-start | bytes 786440 | tf_op jit(solution)/shard_map/ppermute | solution.py:18
  455.5 0.7 copy-start.12
  464.6 65.0 %copy-start.13 = (f32[1,16384]{1,0:T(1,128)S(1)}, f32[1,16384]{1,0:T(1,128)}, u32[]{:S(2)}) copy-start(f32[1,16384]{1,0:T(1,128)} %get-tuple-element.36) | copy-start | bytes 196612
  523.7 6.0 copy-start.14
  536.5 98.0 %copy-start.3 = (f32[6,8192]{1,0:T(8,128)S(1)}, f32[6,8192]{1,0:T(8,128)}, u32[]{:S(2)}) copy-start(f32[6,8192]{1,0:T(8,128)} %copy-done.2) | copy-start | bytes 589828
  536.6 98.0 %copy-start.7 = (f32[6,8192]{1,0:T(8,128)S(1)}, f32[6,8192]{1,0:T(8,128)}, u32[]{:S(2)}) copy-start(f32[6,8192]{1,0:T(8,128)} %param.17) | copy-start | bytes 589828
where the time goes:
time: 637 us; the launch traced here: 635 us
  local copies, waits for them, and re-layouts  338 us (53%)
  other arithmetic  224 us (35%)
  starting transfers between devices  41.7 us (7%)
  waiting for transfers between devices  16.3 us (3%)
  blocking collectives  14 us (2%)
    scatter-add x2, other arithmetic, facet_load(): jax.ops.segment_sum(row, own_idx, num_segments=segments)  180 us
    gather x4, local copies, waits for them, and re-layouts, facet_load(): side_b = window[:, other_idx]  129 us
    gather x4, local copies, waits for them, and re-layouts, facet_load(): side_a = own_rows[:, own_idx]  124 us
    gather x3, local copies, waits for them, and re-layouts, body(): fields = slab.reshape(2, -1)[:, host_cell]  36.6 us
    ppermute x8, starting transfers between devices, padded_2(): lax.ppermute(lax.slice_in_dim(block, block.shape[dim] - width, None, axis...  28.1 us
    concatenate x8, other arithmetic, padded_2(): block = jnp.concatenate([low, block, high], axis=dim)  19.2 us
    ppermute x8, waiting for transfers between devices, padded_2(): lax.ppermute(lax.slice_in_dim(block, 0, width, axis=dim), axis, backward)  16.2 us
    all_gather x1, blocking collectives, body(): gathered = lax.all_gather(state, 'gy', axis=3, tiled=True)  14 us
  transfers between devices with their start and end apart: 16, of which 6 were waited for; matrix products, arithmetic and copies ran while one was open for 22% of the time, Pallas kernels for 0%

commit v1 on v0

v1 whole, which is shorter than its diff:
```python
import functools
import jax
import jax.numpy as jnp
from jax import lax
from jax.sharding import PartitionSpec as P
from jax.experimental import pallas as pl
from jax.experimental.pallas import tpu as pltpu

couple_rate = 0.1
time_step = 0.2
LANES = 128
GROUP = 4
VMEM_LIMIT = 48 * 1024 * 1024


def padded_2(block, sides, width):
    for axis, dim in sides:
        count = lax.axis_size(axis)
        forward = [(i, i + 1) for i in range(count - 1)]
        backward = [(target, source) for source, target in forward]
        low = lax.ppermute(
            lax.slice_in_dim(block, block.shape[dim] - width, None, axis=dim), axis, forward
        )
        high = lax.ppermute(lax.slice_in_dim(block, 0, width, axis=dim), axis, backward)
        block = jnp.concatenate([low, block, high], axis=dim)
    return block


def neighbours(block, axis):
    count = lax.axis_size(axis)
    forward = [(i, i + 1) for i in range(count - 1)]
    backward = [(target, source) for source, target in forward]
    return lax.ppermute(block, axis, forward), lax.ppermute(block, axis, backward)


def advance_plan(extended, rates):
    padded = jnp.pad(extended, ((0, 0), (1, 1), (0, 0), (0, 0)))
    center = padded[:, 1:-1, 1:-1, 1:-1]
    laplace = padded[:, 2:, 1:-1, 1:-1] + padded[:, :-2, 1:-1, 1:-1]
    laplace = laplace + padded[:, 1:-1, 2:, 1:-1] + padded[:, 1:-1, :-2, 1:-1]
    laplace = laplace + padded[:, 1:-1, 1:-1, 2:] + padded[:, 1:-1, 1:-1, :-2] - 6.0 * center
    return center + rates * laplace + couple_rate * (center[::-1] - center)


def pick(row, lanes):
    return jnp.take_along_axis(row, lanes, axis=1, mode="promise_in_bounds")


def lookup(tables, rows, index_vecs):
    lows = [jnp.bitwise_and(ix, LANES - 1) for ix in index_vecs]
    highs = [lax.shift_right_logical(ix, 7) for ix in index_vecs]
    width = len(index_vecs)
    acc = tuple(jnp.zeros((8, LANES), jnp.float32) for _ in range(rows * width))
    base = 0
    for count, load in tables:
        def step(h, acc, load=load, base=base):
            masks = [hi == h + base for hi in highs]
            out = []
            for r in range(rows):
                row = jnp.broadcast_to(load(r, h), (8, LANES))
                for v in range(width):
                    out.append(jnp.where(masks[v], pick(row, lows[v]), acc[r * width + v]))
            return tuple(out)

        acc = lax.fori_loop(0, count, step, acc, unroll=4)
        base += count
    return [[acc[r * width + v] for v in range(width)] for r in range(rows)]


def flat_table(ref):
    def load(r, h):
        return ref[pl.ds(r, 1), pl.ds(pl.multiple_of(h * LANES, LANES), LANES)]

    return ref.shape[1] // LANES, load


def packed_table(ref):
    def load(r, h):
        return ref[r, pl.ds(h, 1), :]

    return ref.shape[1], load


def cross(left, right):
    return [
        left[1] * right[2] - left[2] * right[1],
        left[2] * right[0] - left[0] * right[2],
        left[0] * right[1] - left[1] * right[0],
    ]


def call(kernel, outs, scratch=(), smem=0, count=0, cost=None):
    specs = [pl.BlockSpec(memory_space=pltpu.SMEM)] * smem
    specs += [pl.BlockSpec(memory_space=pltpu.VMEM)] * (count - smem)
    return pl.pallas_call(
        kernel,
        out_shape=outs,
        in_specs=specs,
        out_specs=jax.tree.map(lambda _: pl.BlockSpec(memory_space=pltpu.VMEM), outs),
        scratch_shapes=list(scratch),
        compiler_params=pltpu.CompilerParams(vmem_limit_bytes=VMEM_LIMIT),
        cost_estimate=cost,
    )


def host_kernel(slab_ref, host_ref, out_ref):
    for g in range(host_ref.shape[0] // (8 * GROUP)):
        index = [host_ref[(g * GROUP + v) * 8:(g * GROUP + v + 1) * 8, :] for v in range(GROUP)]
        found = lookup([packed_table(slab_ref)], 2, index)
        for r in range(2):
            for v in range(GROUP):
                out_ref[r, (g * GROUP + v) * 8:(g * GROUP + v + 1) * 8, :] = found[r][v]


def unpack(src, k0, rows, stage):
    for k in range(8 * GROUP):
        at = pl.multiple_of((k0 + k) * LANES, LANES)
        stage[k * rows:(k + 1) * rows, :] = src[:, pl.ds(at, LANES)]
    return [stage[pl.ds(m, 8 * GROUP, stride=rows), :] for m in range(rows)]


def eigen_kernel(own_f, prev_f, next_f, own_ref, other_ref, eigen_ref, out_ref, stage):
    def chunk(g, carry):
        at = pl.multiple_of(g * 8 * GROUP, 8 * GROUP)
        own_ix = [own_ref[pl.ds(at + 8 * v, 8), :] for v in range(GROUP)]
        oth_ix = [other_ref[pl.ds(at + 8 * v, 8), :] for v in range(GROUP)]
        a = lookup([packed_table(own_f)], 2, own_ix)
        b = lookup([packed_table(prev_f), packed_table(own_f), packed_table(next_f)], 2, oth_ix)
        eig = unpack(eigen_ref, at, 2, stage)
        heat = jnp.concatenate([a[1][v] + b[1][v] for v in range(GROUP)], axis=0)
        pore = jnp.concatenate([a[0][v] + b[0][v] for v in range(GROUP)], axis=0)
        out_ref[pl.ds(at, 8 * GROUP), :] = 0.5 * (eig[0] * heat + eig[1] * pore)
        return carry

    lax.fori_loop(0, own_ref.shape[0] // (8 * GROUP), chunk, 0)


def delta_kernel(own_q, prev_q, next_q, own_ref, other_ref, arms_ref, out_ref, stage):
    def chunk(g, carry):
        at = pl.multiple_of(g * 8 * GROUP, 8 * GROUP)
        own_ix = [own_ref[pl.ds(at + 8 * v, 8), :] for v in range(GROUP)]
        oth_ix = [other_ref[pl.ds(at + 8 * v, 8), :] for v in range(GROUP)]
        join = lambda parts: [jnp.concatenate(row, axis=0) for row in parts]
        a = join(lookup([flat_table(own_q)], 6, own_ix))
        b = join(lookup([flat_table(prev_q), flat_table(own_q), flat_table(next_q)], 6, oth_ix))
        arms = unpack(arms_ref, at, 6, stage)
        turn_a = cross(a[3:6], arms[0:3])
        turn_b = cross(b[3:6], arms[3:6])
        for m in range(3):
            out_ref[m, pl.ds(at, 8 * GROUP), :] = (b[m] + turn_b[m]) - (a[m] + turn_a[m])
        return carry

    lax.fori_loop(0, own_ref.shape[0] // (8 * GROUP), chunk, 0)


def update_kernel(live_ref, delta_ref, eig_ref, own_ref, arms_ref, frame_ref, stiff_ref,
                  inertia_ref, disp_ref, vel_ref, disp_out, vel_out,
                  stage, terms, amat, bmat, total):
    blocks = own_ref.shape[0]
    parts = disp_ref.shape[1]
    low_count = 2 * LANES
    high_count = parts // low_count
    per = 8 * GROUP
    live = live_ref[0]
    total[...] = jnp.zeros_like(total)

    def chunk(g, carry):
        at = pl.multiple_of(g * per, per)
        rows = pl.ds(at, per)
        frame = unpack(frame_ref, at, 9, stage)
        delta = [delta_ref[m, rows, :] for m in range(3)]
        e = [frame[3 * k] * delta[0] + frame[3 * k + 1] * delta[1] + frame[3 * k + 2] * delta[2]
             for k in range(3)]
        stiff = unpack(stiff_ref, at, 2, stage)
        block = at + lax.broadcasted_iota(jnp.int32, (per, LANES), 0)
        weight = jnp.where(block < live, 1.0, 0.0).astype(jnp.float32)
        s = [stiff[0] * (e[0] - eig_ref[rows, :]), stiff[1] * e[1], stiff[1] * e[2]]
        force = [(s[0] * frame[m] + s[1] * frame[3 + m] + s[2] * frame[6 + m]) * weight
                 for m in range(3)]
        arms = unpack(arms_ref, at, 6, stage)
        moment = cross(arms[0:3], force)
        for m in range(3):
            terms[m] = force[m]
            terms[3 + m] = moment[m]

        low_iota = lax.broadcasted_iota(jnp.int32, (low_count, LANES), 0)
        high_iota = lax.broadcasted_iota(jnp.int32, (high_count, LANES), 0)
        for k in range(per):
            lanes = pl.ds(k * LANES, LANES)
            ix = own_ref[pl.ds(at + k, 1), :]
            low = jnp.broadcast_to(jnp.bitwise_and(ix, low_count - 1), (low_count, LANES))
            bmat[:, lanes] = jnp.where(low == low_iota, 1.0, 0.0).astype(jnp.bfloat16)
            here = jnp.broadcast_to(lax.shift_right_logical(ix, 8), (high_count, LANES)) == high_iota
            for m in range(6):
                row = terms[m, k:k + 1, :]
                top = row.astype(jnp.bfloat16).astype(jnp.float32)
                rest = row - top
                at_m = m * high_count
                amat[at_m:at_m + high_count, lanes] = jnp.where(
                    here, jnp.broadcast_to(top, here.shape), 0.0).astype(jnp.bfloat16)
                at_m = (6 + m) * high_count
                amat[at_m:at_m + high_count, lanes] = jnp.where(
                    here, jnp.broadcast_to(rest, here.shape), 0.0).astype(jnp.bfloat16)
        total[...] += lax.dot_general(amat[...], bmat[...], (((1,), (1,)), ((), ())),
                                      preferred_element_type=jnp.float32)
        return carry

    lax.fori_loop(0, blocks // per, chunk, 0)
    half = 6 * high_count
    total[0:half, :] = total[0:half, :] + total[half:2 * half, :]
    for h in range(high_count):
        lanes = pl.ds(h * low_count, low_count)
        load = jnp.concatenate([total[m * high_count + h:m * high_count + h + 1, :] for m in range(6)], axis=0)
        mass = jnp.concatenate([jnp.broadcast_to(inertia_ref[0:1, lanes], (3, low_count)),
                                jnp.broadcast_to(inertia_ref[1:2, lanes], (3, low_count))], axis=0)
        vel = vel_ref[:, lanes] + time_step * load / mass
        vel_out[:, lanes] = vel
        disp_out[:, lanes] = disp_ref[:, lanes] + time_step * vel


def body(
    cell_start,
    diffusivity,
    host_cell,
    disp_start,
    vel_start,
    inertia,
    facet_own,
    facet_other,
    facet_arms,
    facet_frame,
    facet_stiffness,
    facet_eigen,
    live_blocks,
):
    f32 = jnp.float32
    facets = facet_own.shape[0]
    blocks = facets // LANES
    particles = disp_start.shape[1]
    own = facet_own.reshape(blocks, LANES)
    other = facet_other.reshape(blocks, LANES)
    per = 8 * GROUP

    state = cell_start
    for substep in range(3):
        extended = padded_2(state, (("gx", 2), ("gy", 3)), 1)
        state = advance_plan(extended, diffusivity)
    layers = state.shape[1]
    slab_rows = layers // lax.axis_size("gy")
    gathered = lax.all_gather(state, "gy", axis=3, tiled=True)
    slab = lax.dynamic_slice_in_dim(gathered, lax.axis_index("gy") * slab_rows, slab_rows, 1)
    slab = slab.reshape(2, -1, LANES)

    fields = call(host_kernel, jax.ShapeDtypeStruct((2, particles // LANES, LANES), f32), count=2)(
        slab, host_cell.reshape(-1, LANES))
    prev_f, next_f = neighbours(fields, "gx")
    eig = call(eigen_kernel, jax.ShapeDtypeStruct((blocks, LANES), f32), count=6,
               scratch=[pltpu.VMEM((per * 2, LANES), f32)])(
        fields, prev_f, next_f, own, other, facet_eigen)

    disp, vel = disp_start, vel_start
    high_count = particles // (2 * LANES)
    for substep in range(2):
        prev_q, next_q = neighbours(disp, "gx")
        delta = call(delta_kernel, jax.ShapeDtypeStruct((3, blocks, LANES), f32), count=6,
                     scratch=[pltpu.VMEM((per * 6, LANES), f32)])(
            disp, prev_q, next_q, own, other, facet_arms)
        disp, vel = call(
            update_kernel,
            (jax.ShapeDtypeStruct(disp.shape, f32), jax.ShapeDtypeStruct(vel.shape, f32)),
            count=10, smem=1,
            scratch=[
                pltpu.VMEM((per * 9, LANES), f32),
                pltpu.VMEM((6, per, LANES), f32),
                pltpu.VMEM((12 * high_count, per * LANES), jnp.bfloat16),
                pltpu.VMEM((2 * LANES, per * LANES), jnp.bfloat16),
                pltpu.VMEM((12 * high_count, 2 * LANES), f32),
            ])(live_blocks, delta, eig, own, facet_arms, facet_frame, facet_stiffness,
               inertia, disp, vel)
    return (state, disp, vel)


def solution(mesh):
    cells = P(None, None, ("groups", "gx"), "gy")
    vector = P(("groups", "gx", "gy"))
    rows = P(None, ("groups", "gx", "gy"))
    return jax.shard_map(
        body,
        mesh=mesh,
        in_specs=(cells, cells, vector, rows, rows, rows, vector, vector, rows, rows, rows, rows,
                  vector),
        out_specs=(cells, rows, rows),
        check_vma=False,
    )
```

time: 637 us -> 328 us (0.51)
  local copies, waits for them, and re-layouts: 338 us -> 2.1 us
  Pallas kernels: 0 us -> 238 us
  other arithmetic: 224 us -> 2.85 us
  starting transfers between devices: 41.7 us -> 51 us
    gather x11 -> x0, local copies, waits for them, and re-layouts: 290 us -> none  [the longest x4 129 us: facet_load(): side_b = window[:, other_idx]]
    pallas_call x0 -> x6, Pallas kernels: none -> 238 us  [the longest x2 171 us: body(): call(delta_kernel, jax.ShapeDtypeStruct((3, blocks, LANES), f32), count=6...]
    scatter-add x2 -> x0, other arithmetic: 180 us -> none  [facet_load(): jax.ops.segment_sum(row, own_idx, num_segments=segments)]
    ppermute x0 -> x6, starting transfers between devices: none -> 17.6 us  [the longest x3 10.8 us: neighbours(): lax.ppermute(block, axis, forward)]
    concatenate x8 -> x6, other arithmetic: 19.2 us -> 1.97 us  [padded_2(): block = jnp.concatenate([low, block, high], axis=dim)]
    concatenate x5 -> x0, local copies, waits for them, and re-layouts: 15.5 us -> none  [the longest x1 7.3 us: padded_2(): block = jnp.concatenate([low, block, high], axis=dim)]
    mul x2 -> x0, local copies, waits for them, and re-layouts: 10.7 us -> none  [facet_load(): terms = jnp.concatenate([force, moment], axis=0) * weight_mask]
    sub x12 -> x0, other arithmetic: 10.5 us -> none  [the longest x2 5.83 us: cross_rows(): left[0] * right[1] - left[1] * right[0]]
  transfers between devices with their start and end apart: 16 -> 18, of which waited for: 6 -> 10; matrix products, arithmetic and copies ran while one was open for 22% -> 0% of each run, Pallas kernels for 0% -> 15%
where the time goes in v1:
time: 328 us; the launch traced here: 327 us
  Pallas kernels  238 us (73%)
  starting transfers between devices  51 us (16%)
  blocking collectives  15.8 us (5%)
  waiting for transfers between devices  15.4 us (5%)
    pallas_call x2, Pallas kernels, body(): call(delta_kernel, jax.ShapeDtypeStruct((3, blocks, LANES), f32), count=6...  171 us
    pallas_call x1, Pallas kernels, body(): call(eigen_kernel, jax.ShapeDtypeStruct((blocks, LANES), f32), count=6, s...  38.9 us
    ppermute x6, starting transfers between devices, padded_2(): lax.ppermute(lax.slice_in_dim(block, block.shape[dim] - width, None, axis...  23.8 us
    pallas_call x2, Pallas kernels, body(): call(update_kernel, (jax.ShapeDtypeStruct(disp.shape, f32), jax.ShapeDtyp...  18.3 us
    all_gather x1, blocking collectives, body(): gathered = lax.all_gather(state, 'gy', axis=3, tiled=True)  15.8 us
    ppermute x3, starting transfers between devices, neighbours(): lax.ppermute(block, axis, forward)  10.8 us
    pallas_call x1, Pallas kernels, body(): call(host_kernel, jax.ShapeDtypeStruct((2, particles // LANES, LANES), f3...  9.72 us
    ppermute x6, starting transfers between devices, padded_2(): lax.ppermute(lax.slice_in_dim(block, 0, width, axis=dim), axis, backward)  9.64 us
  transfers between devices with their start and end apart: 18, of which 10 were waited for; matrix products, arithmetic and copies ran while one was open for 0% of the time, Pallas kernels for 15%

profile of v1, /device:TPU:1, one launch (start us, length us, event | category | flops | bytes accessed | tf_op | source)
XLA Modules:
  0.0 326.8 jit_solution(2119763239626800309)
XLA Ops:
  0.6 1.0 fusion.33
  1.6 4.5 %collective-permute-start = (f32[2,8,1,256]{3,2,1,0:T(1,128)S(1)}, f32[2,8,1,256]{3,2,1,0:T(1,128)S(1)}, u32[]{:S(2)}, u32[]{:S(2)}) collective-permute-start(f32[2,8,1,256]{3,2,1,0:T(1,128)S(1)} %get-tuple-element.21), channel_id=1, source_target_pairs={{0,4},{4,8},{8,12},{1,5},{5,9},{9,13},{2,6},{6,10},{10,14},{3,7},{... | collective-permute-start | bytes 49160 | tf_op jit(solution)/shard_map/ppermute | solution.py:21
  6.2 1.9 collective-permute-start.1
  8.1 0.0 collective-permute-done
  8.1 3.1 collective-permute-done.1
  11.2 1.0 pad_maximum_fusion
  12.2 0.0 copy-start.10
  12.2 0.1 fusion.30
  12.3 1.3 collective-permute-start.3
  13.6 0.0 copy-start.11
  13.6 4.1 %collective-permute-start.2 = (f32[2,8,10,1]{3,2,1,0:T(8,128)S(1)}, f32[2,8,10,1]{3,2,1,0:T(8,128)S(1)}, u32[]{:S(2)}, u32[]{:S(2)}) collective-permute-start(f32[2,8,10,1]{3,2,1,0:T(8,128)S(1)} %get-tuple-element.16), channel_id=1, source_target_pairs={{0,1},{1,2},{2,3},{4,5},{5,6},{6,7},{8,9},{9,10},{10,11},{12,13},{... | collective-permute-start | bytes 1928 | tf_op jit(solution)/shard_map/ppermute | solution.py:21
  17.8 0.3 collective-permute-done.3
  18.0 1.8 collective-permute-done.2
  19.8 0.3 select_maximum_fusion.8
  20.1 0.3 fusion.2
  20.5 2.9 collective-permute-start.4
  23.4 1.9 collective-permute-start.5
  25.3 0.0 collective-permute-done.4
  25.3 3.1 collective-permute-done.5
  28.5 0.1 fusion.29
  28.6 1.3 collective-permute-start.7
  29.9 4.7 %collective-permute-start.6 = (f32[2,8,10,1]{3,2,1,0:T(8,128)S(1)}, f32[2,8,10,1]{3,2,1,0:T(8,128)S(1)}, u32[]{:S(2)}, u32[]{:S(2)}) collective-permute-start(f32[2,8,10,1]{3,2,1,0:T(8,128)S(1)} %get-tuple-element.14), channel_id=1, source_target_pairs={{0,1},{1,2},{2,3},{4,5},{5,6},{6,7},{8,9},{9,10},{10,11},{12,13},{... | collective-permute-start | bytes 1928 | tf_op jit(solution)/shard_map/ppermute | solution.py:21
  34.6 0.4 collective-permute-done.7
  35.0 1.5 collective-permute-done.6
  36.5 0.3 select_maximum_fusion.4
  36.9 0.0 copy-start.3
  36.9 0.3 fusion.4
  37.2 2.8 collective-permute-start.8
  40.0 1.9 collective-permute-start.9
  41.9 1.9 collective-permute-start.13
  43.9 0.0 collective-permute-done.8
  43.9 1.2 collective-permute-done.9
  45.1 0.1 fusion.28
  45.2 1.3 collective-permute-start.11
  46.5 4.7 %collective-permute-start.10 = (f32[2,8,10,1]{3,2,1,0:T(8,128)S(1)}, f32[2,8,10,1]{3,2,1,0:T(8,128)S(1)}, u32[]{:S(2)}, u32[]{:S(2)}) collective-permute-start(f32[2,8,10,1]{3,2,1,0:T(8,128)S(1)} %get-tuple-element.12), channel_id=1, source_target_pairs={{0,1},{1,2},{2,3},{4,5},{5,6},{6,7},{8,9},{9,10},{10,11},{12,13},{... | collective-permute-start | bytes 1928 | tf_op jit(solution)/shard_map/ppermute | solution.py:21
  51.2 2.8 collective-permute-start.12
  54.0 0.0 collective-permute-done.11
  54.0 0.0 collective-permute-done.10
  54.0 0.3 select_maximum_fusion
  54.3 0.3 fusion.6
  54.6 0.0 copy-start.12
  54.6 15.8 %all_gather.3 = f32[2,8,8,1024]{3,2,1,0:T(8,128)S(1)} all-gather(f32[2,8,8,256]{3,2,1,0:T(8,128)S(1)} %fusion.6), channel_id=1, replica_groups=mesh['groups'=2,'gx'=4,'gy'=4] {'gy'}, dimensions={3}, use_global_device_ids=true | all-gather | bytes 655360 | tf_op jit(solution)/shard_map/all_gather | solution.py:250
  70.5 0.0 copy-start.4
  70.5 0.0 copy-start.8
  70.5 0.0 copy-start
  70.6 0.7 copy-done.9
  71.2 9.7 %shard_map.149.own_f = f32[2,64,128]{2,1,0:T(8,128)S(1)} custom-call(f32[2,128,128]{2,1,0:T(8,128)S(1)} %reshape.20.slab_ref, s32[64,128]{1,0:T(8,128)S(1)} %bitcast.13), custom_call_target="tpu_custom_call" | custom-call | tf_op jit(solution)/shard_map/pallas_call | solution.py:254
  81.0 2.9 collective-permute-start.15
  83.9 3.8 %collective-permute-start.14 = (f32[2,64,128]{2,1,0:T(8,128)S(1)}, f32[2,64,128]{2,1,0:T(8,128)S(1)}, u32[]{:S(2)}, u32[]{:S(2)}) collective-permute-start(f32[2,64,128]{2,1,0:T(8,128)S(1)} %shard_map.149.own_f), channel_id=1, source_target_pairs={{0,4},{4,8},{8,12},{1,5},{5,9},{9,13},{2,6},{6,10},{10,14},{3,7},{... | collective-permute-start | bytes 196616 | tf_op jit(solution)/shard_map/ppermute | solution.py:33
  88.3 0.0 collective-permute-done.15.next_f
  88.4 0.7 collective-permute-done.14.prev_f
  89.0 38.9 %shard_map.150.eig_ref = f32[128,128]{1,0:T(8,128)S(1)} custom-call(f32[2,64,128]{2,1,0:T(8,128)S(1)} %shard_map.149.own_f, f32[2,64,128]{2,1,0:T(8,128)S(1)} %collective-permute-done.14.prev_f, f32[2,64,128]{2,1,0:T(8,128)S(1)} %collective-permute-done.15.next_f, s32[128,128]{1,0:T(8,128)S(1)} %bitcast.5, s32[128,128]{1,0:T(8,128)S(1)} %bitcast.10, ...), custom_call_target="tpu_custom_call" | custom-call | tf_op jit(solution)/shard_map/pallas_call | solution.py:257
  127.9 0.0 copy-start.5
  128.0 0.0 copy-start.6
  128.0 0.0 copy-start.7
  128.0 0.0 collective-permute-done.13.next_q
  128.0 85.5 %shard_map.148.delta_ref = f32[3,128,128]{2,1,0:T(8,128)S(1)} custom-call(f32[6,8192]{1,0:T(8,128)S(1)} %copy-done.3, f32[6,8192]{1,0:T(8,128)S(1)} %collective-permute-done.12.prev_q, f32[6,8192]{1,0:T(8,128)S(1)} %collective-permute-done.13.next_q, s32[128,128]{1,0:T(8,128)S(1)} %bitcast.6, s32[128,128]{1,0:T(8,128)S(1)} %bitcast.11, f32[6,16384]{1,0:T(8,128)S(1)} %copy-done), custom_call_target="tpu_custom_call" | custom-call | tf_op jit(solution)/shard_map/pallas_call | solution.py:265
  213.6 8.7 %shard_map.151 = (f32[6,8192]{1,0:T(8,128)S(1)}, f32[6,8192]{1,0:T(8,128)S(1)}) custom-call(s32[1]{0:T(128)S(6)} %copy.16.live_ref, f32[3,128,128]{2,1,0:T(8,128)S(1)} %shard_map.148.delta_ref, f32[128,128]{1,0:T(8,128)S(1)} %shard_map.150.eig_ref, s32[128,128]{1,0:T(8,128)S(1)} %bitcast.7, f32[6,16384]{1,0:T(8,128)S(1)} %copy-done, ...), custom_call_target="tpu_custom_call" | custom-call | tf_op jit(solution)/shard_map/pallas_call | solution.py:268
  222.3 1.9 collective-permute-start.17
  224.2 4.3 %collective-permute-start.16 = (f32[6,8192]{1,0:T(8,128)S(1)}, f32[6,8192]{1,0:T(8,128)S(1)}, u32[]{:S(2)}, u32[]{:S(2)}) collective-permute-start(f32[6,8192]{1,0:T(8,128)S(1)} %get-tuple-element.7.own_q.disp_ref), channel_id=1, source_target_pairs={{0,4},{4,8},{8,12},{1,5},{5,9},{9,13},{2,6},{6,10},{10,14},{3,7},{... | collective-permute-start | bytes 589832 | tf_op jit(solution)/shard_map/ppermute | solution.py:33
  228.5 2.1 collective-permute-done.17.next_q
  230.6 1.2 collective-permute-done.16.prev_q
  231.8 85.5 %shard_map.152.delta_ref = f32[3,128,128]{2,1,0:T(8,128)S(1)} custom-call(f32[6,8192]{1,0:T(8,128)S(1)} %get-tuple-element.7.own_q.disp_ref, f32[6,8192]{1,0:T(8,128)S(1)} %collective-permute-done.16.prev_q, f32[6,8192]{1,0:T(8,128)S(1)} %collective-permute-done.17.next_q, s32[128,128]{1,0:T(8,128)S(1)} %bitcast.8, s32[128,128]{1,0:T(8,128)S(1)} %bitcast.12, ...), custom_call_target="tpu_custom_call" | custom-call | tf_op jit(solution)/shard_map/pallas_call | solution.py:265
  317.3 9.5 %shard_map.153 = (f32[6,8192]{1,0:T(8,128)}, f32[6,8192]{1,0:T(8,128)}) custom-call(s32[1]{0:T(128)S(6)} %copy.16.live_ref, f32[3,128,128]{2,1,0:T(8,128)S(1)} %shard_map.152.delta_ref, f32[128,128]{1,0:T(8,128)S(1)} %shard_map.150.eig_ref, s32[128,128]{1,0:T(8,128)S(1)} %bitcast.9, f32[6,16384]{1,0:T(8,128)S(1)} %copy-done, f32[9,16384]{1,0:T(8,128)S(1)} %copy-done.1, ...), custom_call_target="tpu_custom_call" | custom-call | tf_op jit(solution)/shard_map/pallas_call | solution.py:268
  (22 shorter events, 0.2 us)
Async XLA Ops:
  1.6 6.5 %collective-permute-start = (f32[2,8,1,256]{3,2,1,0:T(1,128)S(1)}, f32[2,8,1,256]{3,2,1,0:T(1,128)S(1)}, u32[]{:S(2)}, u32[]{:S(2)}) collective-permute-start(f32[2,8,1,256]{3,2,1,0:T(1,128)S(1)} %get-tuple-element.21), channel_id=1, source_target_pairs={{0,4},{4,8},{8,12},{1,5},{5,9},{9,13},{2,6},{6,10},{10,14},{3,7},{... | collective-permute-start | bytes 49160 | tf_op jit(solution)/shard_map/ppermute | solution.py:21
  6.2 5.1 %collective-permute-start.1 = (f32[2,8,1,256]{3,2,1,0:T(1,128)S(1)}, f32[2,8,1,256]{3,2,1,0:T(1,128)S(1)}, u32[]{:S(2)}, u32[]{:S(2)}) collective-permute-start(f32[2,8,1,256]{3,2,1,0:T(1,128)S(1)} %get-tuple-element.22), channel_id=1, source_target_pairs={{4,0},{8,4},{12,8},{5,1},{9,5},{13,9},{6,2},{10,6},{14,10},{7,3},{... | collective-permute-start | bytes 49160 | tf_op jit(solution)/shard_map/ppermute | solution.py:24
  12.2 7.6 %copy-start.10 = (f32[2,8,8,256]{3,2,1,0:T(8,128)S(1)}, f32[2,8,8,256]{3,2,1,0:T(8,128)}, u32[]{:S(2)}) copy-start(f32[2,8,8,256]{3,2,1,0:T(8,128)} %param.13) | copy-start | bytes 393220
  12.3 5.7 %collective-permute-start.3 = (f32[2,8,10,1]{3,2,1,0:T(8,128)S(1)}, f32[2,8,10,1]{3,2,1,0:T(8,128)S(1)}, u32[]{:S(2)}, u32[]{:S(2)}) collective-permute-start(f32[2,8,10,1]{3,2,1,0:T(8,128)S(1)} %get-tuple-element.15), channel_id=1, source_target_pairs={{1,0},{2,1},{3,2},{5,4},{6,5},{7,6},{9,8},{10,9},{11,10},{13,12},{... | collective-permute-start | bytes 1928 | tf_op jit(solution)/shard_map/ppermute | solution.py:24
  13.6 6.5 %copy-start.11 = (f32[2,8,8,256]{3,2,1,0:T(8,128)S(1)}, f32[2,8,8,256]{3,2,1,0:T(8,128)}, u32[]{:S(2)}) copy-start(f32[2,8,8,256]{3,2,1,0:T(8,128)} %param.14) | copy-start | bytes 393220
  13.6 6.2 %collective-permute-start.2 = (f32[2,8,10,1]{3,2,1,0:T(8,128)S(1)}, f32[2,8,10,1]{3,2,1,0:T(8,128)S(1)}, u32[]{:S(2)}, u32[]{:S(2)}) collective-permute-start(f32[2,8,10,1]{3,2,1,0:T(8,128)S(1)} %get-tuple-element.16), channel_id=1, source_target_pairs={{0,1},{1,2},{2,3},{4,5},{5,6},{6,7},{8,9},{9,10},{10,11},{12,13},{... | collective-permute-start | bytes 1928 | tf_op jit(solution)/shard_map/ppermute | solution.py:21
  20.5 4.9 %collective-permute-start.4 = (f32[2,8,1,256]{3,2,1,0:T(1,128)S(1)}, f32[2,8,1,256]{3,2,1,0:T(1,128)S(1)}, u32[]{:S(2)}, u32[]{:S(2)}) collective-permute-start(f32[2,8,1,256]{3,2,1,0:T(1,128)S(1)} %get-tuple-element.19), channel_id=1, source_target_pairs={{0,4},{4,8},{8,12},{1,5},{5,9},{9,13},{2,6},{6,10},{10,14},{3,7},{... | collective-permute-start | bytes 49160 | tf_op jit(solution)/shard_map/ppermute | solution.py:21
  23.4 5.1 %collective-permute-start.5 = (f32[2,8,1,256]{3,2,1,0:T(1,128)S(1)}, f32[2,8,1,256]{3,2,1,0:T(1,128)S(1)}, u32[]{:S(2)}, u32[]{:S(2)}) collective-permute-start(f32[2,8,1,256]{3,2,1,0:T(1,128)S(1)} %get-tuple-element.20), channel_id=1, source_target_pairs={{4,0},{8,4},{12,8},{5,1},{9,5},{13,9},{6,2},{10,6},{14,10},{7,3},{... | collective-permute-start | bytes 49160 | tf_op jit(solution)/shard_map/ppermute | solution.py:24
  28.6 6.4 %collective-permute-start.7 = (f32[2,8,10,1]{3,2,1,0:T(8,128)S(1)}, f32[2,8,10,1]{3,2,1,0:T(8,128)S(1)}, u32[]{:S(2)}, u32[]{:S(2)}) collective-permute-start(f32[2,8,10,1]{3,2,1,0:T(8,128)S(1)} %get-tuple-element.13), channel_id=1, source_target_pairs={{1,0},{2,1},{3,2},{5,4},{6,5},{7,6},{9,8},{10,9},{11,10},{13,12},{... | collective-permute-start | bytes 1928 | tf_op jit(solution)/shard_map/ppermute | solution.py:24
  29.9 6.6 %collective-permute-start.6 = (f32[2,8,10,1]{3,2,1,0:T(8,128)S(1)}, f32[2,8,10,1]{3,2,1,0:T(8,128)S(1)}, u32[]{:S(2)}, u32[]{:S(2)}) collective-permute-start(f32[2,8,10,1]{3,2,1,0:T(8,128)S(1)} %get-tuple-element.14), channel_id=1, source_target_pairs={{0,1},{1,2},{2,3},{4,5},{5,6},{6,7},{8,9},{9,10},{10,11},{12,13},{... | collective-permute-start | bytes 1928 | tf_op jit(solution)/shard_map/ppermute | solution.py:21
  36.9 5.1 %copy-start.3 = (f32[6,8192]{1,0:T(8,128)S(1)}, f32[6,8192]{1,0:T(8,128)}, u32[]{:S(2)}) copy-start(f32[6,8192]{1,0:T(8,128)} %disp_ref.1) | copy-start | bytes 589828
  37.2 6.7 %collective-permute-start.8 = (f32[2,8,1,256]{3,2,1,0:T(1,128)S(1)}, f32[2,8,1,256]{3,2,1,0:T(1,128)S(1)}, u32[]{:S(2)}, u32[]{:S(2)}) collective-permute-start(f32[2,8,1,256]{3,2,1,0:T(1,128)S(1)} %get-tuple-element.17), channel_id=1, source_target_pairs={{0,4},{4,8},{8,12},{1,5},{5,9},{9,13},{2,6},{6,10},{10,14},{3,7},{... | collective-permute-start | bytes 49160 | tf_op jit(solution)/shard_map/ppermute | solution.py:21
  40.0 5.1 %collective-permute-start.9 = (f32[2,8,1,256]{3,2,1,0:T(1,128)S(1)}, f32[2,8,1,256]{3,2,1,0:T(1,128)S(1)}, u32[]{:S(2)}, u32[]{:S(2)}) collective-permute-start(f32[2,8,1,256]{3,2,1,0:T(1,128)S(1)} %get-tuple-element.18), channel_id=1, source_target_pairs={{4,0},{8,4},{12,8},{5,1},{9,5},{13,9},{6,2},{10,6},{14,10},{7,3},{... | collective-permute-start | bytes 49160 | tf_op jit(solution)/shard_map/ppermute | solution.py:24
  41.9 86.0 %collective-permute-start.13 = (f32[6,8192]{1,0:T(8,128)S(1)}, f32[6,8192]{1,0:T(8,128)S(1)}, u32[]{:S(2)}, u32[]{:S(2)}) collective-permute-start(f32[6,8192]{1,0:T(8,128)S(1)} %copy-done.3), channel_id=1, source_target_pairs={{4,0},{8,4},{12,8},{5,1},{9,5},{13,9},{6,2},{10,6},{14,10},{7,3},{... | collective-permute-start | bytes 589832 | tf_op jit(solution)/shard_map/ppermute | solution.py:33
  45.2 8.8 %collective-permute-start.11 = (f32[2,8,10,1]{3,2,1,0:T(8,128)S(1)}, f32[2,8,10,1]{3,2,1,0:T(8,128)S(1)}, u32[]{:S(2)}, u32[]{:S(2)}) collective-permute-start(f32[2,8,10,1]{3,2,1,0:T(8,128)S(1)} %get-tuple-element.11), channel_id=1, source_target_pairs={{1,0},{2,1},{3,2},{5,4},{6,5},{7,6},{9,8},{10,9},{11,10},{13,12},{... | collective-permute-start | bytes 1928 | tf_op jit(solution)/shard_map/ppermute | solution.py:24
  46.5 7.5 %collective-permute-start.10 = (f32[2,8,10,1]{3,2,1,0:T(8,128)S(1)}, f32[2,8,10,1]{3,2,1,0:T(8,128)S(1)}, u32[]{:S(2)}, u32[]{:S(2)}) collective-permute-start(f32[2,8,10,1]{3,2,1,0:T(8,128)S(1)} %get-tuple-element.12), channel_id=1, source_target_pairs={{0,1},{1,2},{2,3},{4,5},{5,6},{6,7},{8,9},{9,10},{10,11},{12,13},{... | collective-permute-start | bytes 1928 | tf_op jit(solution)/shard_map/ppermute | solution.py:21
  51.2 76.8 %collective-permute-start.12 = (f32[6,8192]{1,0:T(8,128)S(1)}, f32[6,8192]{1,0:T(8,128)S(1)}, u32[]{:S(2)}, u32[]{:S(2)}) collective-permute-start(f32[6,8192]{1,0:T(8,128)S(1)} %copy-done.3), channel_id=1, source_target_pairs={{0,4},{4,8},{8,12},{1,5},{5,9},{9,13},{2,6},{6,10},{10,14},{3,7},{... | collective-permute-start | bytes 589832 | tf_op jit(solution)/shard_map/ppermute | solution.py:33
  54.6 15.8 %copy-start.12 = (f32[2,8,8,256]{3,2,1,0:T(8,128)}, f32[2,8,8,256]{3,2,1,0:T(8,128)S(1)}, u32[]{:S(2)}) copy-start(f32[2,8,8,256]{3,2,1,0:T(8,128)S(1)} %fusion.6) | copy-start | bytes 393220
  70.5 0.8 copy-start.9
  70.5 18.5 %copy-start.2 = (s32[16384]{0:T(1024)S(1)}, s32[16384]{0:T(1024)}, u32[]{:S(2)}) copy-start(s32[16384]{0:T(1024)} %param.19) | copy-start | bytes 196612
  70.5 18.5 %copy-start.4 = (s32[16384]{0:T(1024)S(1)}, s32[16384]{0:T(1024)}, u32[]{:S(2)}) copy-start(s32[16384]{0:T(1024)} %param.20) | copy-start | bytes 196612
  70.5 18.5 %copy-start.8 = (f32[2,16384]{1,0:T(2,128)S(1)}, f32[2,16384]{1,0:T(2,128)}, u32[]{:S(2)}) copy-start(f32[2,16384]{1,0:T(2,128)} %eigen_ref.1) | copy-start | bytes 393220
  70.5 57.5 %copy-start = (f32[6,16384]{1,0:T(8,128)S(1)}, f32[6,16384]{1,0:T(8,128)}, u32[]{:S(2)}) copy-start(f32[6,16384]{1,0:T(8,128)} %arms_ref.7) | copy-start | bytes 1179652
  81.0 7.4 %collective-permute-start.15 = (f32[2,64,128]{2,1,0:T(8,128)S(1)}, f32[2,64,128]{2,1,0:T(8,128)S(1)}, u32[]{:S(2)}, u32[]{:S(2)}) collective-permute-start(f32[2,64,128]{2,1,0:T(8,128)S(1)} %shard_map.149.own_f), channel_id=1, source_target_pairs={{4,0},{8,4},{12,8},{5,1},{9,5},{13,9},{6,2},{10,6},{14,10},{7,3},{... | collective-permute-start | bytes 196616 | tf_op jit(solution)/shard_map/ppermute | solution.py:33
  83.9 5.1 %collective-permute-start.14 = (f32[2,64,128]{2,1,0:T(8,128)S(1)}, f32[2,64,128]{2,1,0:T(8,128)S(1)}, u32[]{:S(2)}, u32[]{:S(2)}) collective-permute-start(f32[2,64,128]{2,1,0:T(8,128)S(1)} %shard_map.149.own_f), channel_id=1, source_target_pairs={{0,4},{4,8},{8,12},{1,5},{5,9},{9,13},{2,6},{6,10},{10,14},{3,7},{... | collective-permute-start | bytes 196616 | tf_op jit(solution)/shard_map/ppermute | solution.py:33
  89.0 124.5 %copy-start.1 = (f32[9,16384]{1,0:T(8,128)S(1)}, f32[9,16384]{1,0:T(8,128)}, u32[]{:S(2)}) copy-start(f32[9,16384]{1,0:T(8,128)} %frame_ref.3) | copy-start | bytes 1769476
  127.9 85.6 %copy-start.5 = (f32[2,16384]{1,0:T(2,128)S(1)}, f32[2,16384]{1,0:T(2,128)}, u32[]{:S(2)}) copy-start(f32[2,16384]{1,0:T(2,128)} %stiff_ref.3) | copy-start | bytes 393220
  128.0 85.6 %copy-start.6 = (f32[2,8192]{1,0:T(2,128)S(1)}, f32[2,8192]{1,0:T(2,128)}, u32[]{:S(2)}) copy-start(f32[2,8192]{1,0:T(2,128)} %inertia_ref.3) | copy-start | bytes 196612
  128.0 85.6 %copy-start.7 = (f32[6,8192]{1,0:T(8,128)S(1)}, f32[6,8192]{1,0:T(8,128)}, u32[]{:S(2)}) copy-start(f32[6,8192]{1,0:T(8,128)} %vel_ref.1) | copy-start | bytes 589828
  222.3 8.3 %collective-permute-start.17 = (f32[6,8192]{1,0:T(8,128)S(1)}, f32[6,8192]{1,0:T(8,128)S(1)}, u32[]{:S(2)}, u32[]{:S(2)}) collective-permute-start(f32[6,8192]{1,0:T(8,128)S(1)} %get-tuple-element.7.own_q.disp_ref), channel_id=1, source_target_pairs={{4,0},{8,4},{12,8},{5,1},{9,5},{13,9},{6,2},{10,6},{14,10},{7,3},{... | collective-permute-start | bytes 589832 | tf_op jit(solution)/shard_map/ppermute | solution.py:33
  224.2 7.6 %collective-permute-start.16 = (f32[6,8192]{1,0:T(8,128)S(1)}, f32[6,8192]{1,0:T(8,128)S(1)}, u32[]{:S(2)}, u32[]{:S(2)}) collective-permute-start(f32[6,8192]{1,0:T(8,128)S(1)} %get-tuple-element.7.own_q.disp_ref), channel_id=1, source_target_pairs={{0,4},{4,8},{8,12},{1,5},{5,9},{9,13},{2,6},{6,10},{10,14},{3,7},{... | collective-permute-start | bytes 589832 | tf_op jit(solution)/shard_map/ppermute | solution.py:33

commit v2 on v1

--- a/solution.py
+++ b/solution.py
@@ -42,43 +42,57 @@
     return center + rates * laplace + couple_rate * (center[::-1] - center)
 
 
-def pick(row, lanes):
-    return jnp.take_along_axis(row, lanes, axis=1, mode="promise_in_bounds")
-
-
-def lookup(tables, rows, index_vecs):
-    lows = [jnp.bitwise_and(ix, LANES - 1) for ix in index_vecs]
-    highs = [lax.shift_right_logical(ix, 7) for ix in index_vecs]
-    width = len(index_vecs)
-    acc = tuple(jnp.zeros((8, LANES), jnp.float32) for _ in range(rows * width))
+WIDE = 256
+
+
+def fill_table(table, staged, sources, rows):
+    total = staged.shape[0] // rows
     base = 0
-    for count, load in tables:
-        def step(h, acc, load=load, base=base):
-            masks = [hi == h + base for hi in highs]
-            out = []
+    for ref in sources:
+        if len(ref.shape) == 3:
+            count = ref.shape[1]
             for r in range(rows):
-                row = jnp.broadcast_to(load(r, h), (8, LANES))
-                for v in range(width):
-                    out.append(jnp.where(masks[v], pick(row, lows[v]), acc[r * width + v]))
-            return tuple(out)
-
-        acc = lax.fori_loop(0, count, step, acc, unroll=4)
+                staged[r * total + base:r * total + base + count, :] = ref[r]
+        else:
+            count = ref.shape[1] // LANES
+            for h in range(count):
+                staged[pl.ds(base + h, rows, stride=total), :] = ref[:, h * LANES:(h + 1) * LANES]
         base += count
-    return [[acc[r * width + v] for v in range(width)] for r in range(rows)]
-
-
-def flat_table(ref):
-    def load(r, h):
-        return ref[pl.ds(r, 1), pl.ds(pl.multiple_of(h * LANES, LANES), LANES)]
-
-    return ref.shape[1] // LANES, load
-
-
-def packed_table(ref):
-    def load(r, h):
-        return ref[r, pl.ds(h, 1), :]
-
-    return ref.shape[1], load
+    value = staged[...]
+    top = value.astype(jnp.bfloat16)
+    table[:, 0:LANES] = top
+    table[:, LANES:2 * LANES] = (value - top.astype(jnp.float32)).astype(jnp.bfloat16)
+
+
+def look(table, rows, index_row, out, at):
+    total = table.shape[0] // rows
+    low = jnp.broadcast_to(jnp.bitwise_and(index_row, LANES - 1), (LANES, WIDE))
+    hot = jnp.where(low == lax.broadcasted_iota(jnp.int32, (LANES, WIDE), 0), 1.0, 0.0)
+    hot = hot.astype(jnp.bfloat16)
+    found = jnp.dot(table[...], jnp.concatenate([hot, hot], axis=0), preferred_element_type=jnp.float32)
+    high = jnp.broadcast_to(lax.shift_right_logical(index_row, 7), (8, WIDE))
+    high = high - lax.broadcasted_iota(jnp.int32, (8, WIDE), 0)
+    acc = [jnp.zeros((8, WIDE), jnp.float32) for _ in range(rows)]
+    for hb in range(total // 8):
+        mask = high == 8 * hb
+        for r in range(rows):
+            first = r * total + 8 * hb
+            acc[r] = jnp.where(mask, found[first:first + 8, :], acc[r])
+    for r in range(rows):
+        for k in range(WIDE // LANES):
+            out[r, pl.ds(at + 8 * k, 8), :] = acc[r][:, k * LANES:(k + 1) * LANES]
+
+
+def index_of(ref, g):
+    per = WIDE // LANES
+    return jnp.concatenate([ref[pl.ds(g * per + k, 1), :] for k in range(per)], axis=1)
+
+
+def gathered_row(out, r, first, count):
+    parts = [out[r, pl.ds(first * 8 + s, count, stride=8), :] for s in range(8)]
+    while len(parts) > 1:
+        parts = [x + y for x, y in zip(parts[::2], parts[1::2])]
+    return parts[0]
 
 
 def cross(left, right):
@@ -103,13 +117,17 @@
     )
 
 
-def host_kernel(slab_ref, host_ref, out_ref):
-    for g in range(host_ref.shape[0] // (8 * GROUP)):
-        index = [host_ref[(g * GROUP + v) * 8:(g * GROUP + v + 1) * 8, :] for v in range(GROUP)]
-        found = lookup([packed_table(slab_ref)], 2, index)
-        for r in range(2):
-            for v in range(GROUP):
-                out_ref[r, (g * GROUP + v) * 8:(g * GROUP + v + 1) * 8, :] = found[r][v]
+def host_kernel(slab_ref, host_ref, out_ref, staged, table, found):
+    fill_table(table, staged, [slab_ref], 2)
+
+    def chunk(g, carry):
+        look(table, 2, index_of(host_ref, g), found, pl.multiple_of(g * 8 * (WIDE // LANES), 8))
+        return carry
+
+    blocks = host_ref.shape[0]
+    lax.fori_loop(0, blocks * LANES // WIDE, chunk, 0)
+    for r in range(2):
+        out_ref[r] = gathered_row(found, r, 0, blocks)
 
 
 def unpack(src, k0, rows, stage):
@@ -119,30 +137,43 @@
     return [stage[pl.ds(m, 8 * GROUP, stride=rows), :] for m in range(rows)]
 
 
-def eigen_kernel(own_f, prev_f, next_f, own_ref, other_ref, eigen_ref, out_ref, stage):
+def find_both(rows, own_ref, other_ref, own_q, prev_q, next_q, scratch):
+    staged_a, table_a, found_a, staged_b, table_b, found_b = scratch
+    fill_table(table_a, staged_a, [own_q], rows)
+    fill_table(table_b, staged_b, [prev_q, own_q, next_q], rows)
+
+    def chunk(g, carry):
+        at = pl.multiple_of(g * 8 * (WIDE // LANES), 8)
+        look(table_a, rows, index_of(own_ref, g), found_a, at)
+        look(table_b, rows, index_of(other_ref, g), found_b, at)
+        return carry
+
+    lax.fori_loop(0, own_ref.shape[0] * LANES // WIDE, chunk, 0)
+    return found_a, found_b
+
+
+def eigen_kernel(own_f, prev_f, next_f, own_ref, other_ref, eigen_ref, out_ref, stage, *scratch):
+    found_a, found_b = find_both(2, own_ref, other_ref, own_f, prev_f, next_f, scratch)
+
     def chunk(g, carry):
         at = pl.multiple_of(g * 8 * GROUP, 8 * GROUP)
-        own_ix = [own_ref[pl.ds(at + 8 * v, 8), :] for v in range(GROUP)]
-        oth_ix = [other_ref[pl.ds(at + 8 * v, 8), :] for v in range(GROUP)]
-        a = lookup([packed_table(own_f)], 2, own_ix)
-        b = lookup([packed_table(prev_f), packed_table(own_f), packed_table(next_f)], 2, oth_ix)
         eig = unpack(eigen_ref, at, 2, stage)
-        heat = jnp.concatenate([a[1][v] + b[1][v] for v in range(GROUP)], axis=0)
-        pore = jnp.concatenate([a[0][v] + b[0][v] for v in range(GROUP)], axis=0)
+        pore, heat = [
+            gathered_row(found_a, r, at, 8 * GROUP) + gathered_row(found_b, r, at, 8 * GROUP)
+            for r in range(2)]
         out_ref[pl.ds(at, 8 * GROUP), :] = 0.5 * (eig[0] * heat + eig[1] * pore)
         return carry
 
     lax.fori_loop(0, own_ref.shape[0] // (8 * GROUP), chunk, 0)
 
 
-def delta_kernel(own_q, prev_q, next_q, own_ref, other_ref, arms_ref, out_ref, stage):
+def delta_kernel(own_q, prev_q, next_q, own_ref, other_ref, arms_ref, out_ref, stage, *scratch):
+    found_a, found_b = find_both(6, own_ref, other_ref, own_q, prev_q, next_q, scratch)
+
     def chunk(g, carry):
         at = pl.multiple_of(g * 8 * GROUP, 8 * GROUP)
-        own_ix = [own_ref[pl.ds(at + 8 * v, 8), :] for v in range(GROUP)]
-        oth_ix = [other_ref[pl.ds(at + 8 * v, 8), :] for v in range(GROUP)]
-        join = lambda parts: [jnp.concatenate(row, axis=0) for row in parts]
-        a = join(lookup([flat_table(own_q)], 6, own_ix))
-        b = join(lookup([flat_table(prev_q), flat_table(own_q), flat_table(next_q)], 6, oth_ix))
+        a = [gathered_row(found_a, r, at, 8 * GROUP) for r in range(6)]
+        b = [gathered_row(found_b, r, at, 8 * GROUP) for r in range(6)]
         arms = unpack(arms_ref, at, 6, stage)
         turn_a = cross(a[3:6], arms[0:3])
         turn_b = cross(b[3:6], arms[3:6])
@@ -251,11 +282,19 @@
     slab = lax.dynamic_slice_in_dim(gathered, lax.axis_index("gy") * slab_rows, slab_rows, 1)
     slab = slab.reshape(2, -1, LANES)
 
-    fields = call(host_kernel, jax.ShapeDtypeStruct((2, particles // LANES, LANES), f32), count=2)(
+    def tables(rows, high, found):
+        return [pltpu.VMEM((rows * high, LANES), f32),
+                pltpu.VMEM((rows * high, 2 * LANES), jnp.bfloat16),
+                pltpu.VMEM((rows, 8 * found, LANES), f32)]
+
+    high = particles // LANES
+    fields = call(host_kernel, jax.ShapeDtypeStruct((2, high, LANES), f32), count=2,
+                  scratch=tables(2, slab.shape[1], high))(
         slab, host_cell.reshape(-1, LANES))
     prev_f, next_f = neighbours(fields, "gx")
     eig = call(eigen_kernel, jax.ShapeDtypeStruct((blocks, LANES), f32), count=6,
-               scratch=[pltpu.VMEM((per * 2, LANES), f32)])(
+               scratch=[pltpu.VMEM((per * 2, LANES), f32)] + tables(2, high, blocks)
+               + tables(2, 3 * high, blocks))(
         fields, prev_f, next_f, own, other, facet_eigen)
 
     disp, vel = disp_start, vel_start
@@ -263,7 +302,8 @@
     for substep in range(2):
         prev_q, next_q = neighbours(disp, "gx")
         delta = call(delta_kernel, jax.ShapeDtypeStruct((3, blocks, LANES), f32), count=6,
-                     scratch=[pltpu.VMEM((per * 6, LANES), f32)])(
+                     scratch=[pltpu.VMEM((per * 6, LANES), f32)] + tables(6, high, blocks)
+                     + tables(6, 3 * high, blocks))(
             disp, prev_q, next_q, own, other, facet_arms)
         disp, vel = call(
             update_kernel,

time: 328 us -> 183 us (0.56)
  Pallas kernels: 238 us -> 92.6 us
    pallas_call x2, Pallas kernels: 171 us -> 51.9 us  [body(): call(delta_kernel, jax.ShapeDtypeStruct((3, blocks, LANES), f32), count=6...]
    pallas_call x1, Pallas kernels: 38.9 us -> 16.1 us  [body(): call(eigen_kernel, jax.ShapeDtypeStruct((blocks, LANES), f32), count=6, s...]
    pallas_call x1, Pallas kernels: 9.72 us -> 6.3 us  [body(): call(host_kernel, jax.ShapeDtypeStruct((2, high, LANES), f32), count=2, s...]
  transfers between devices with their start and end apart: 18 -> 18, of which waited for: 10 -> 10; matrix products, arithmetic and copies ran while one was open for 0% -> 0% of each run, Pallas kernels for 15% -> 12%
where the time goes in v2:
time: 183 us; the launch traced here: 182 us
  Pallas kernels  92.6 us (51%)
  starting transfers between devices  51 us (28%)
  blocking collectives  15.8 us (9%)
  waiting for transfers between devices  15.4 us (8%)
  other arithmetic  2.85 us (2%)
  local copies, waits for them, and re-layouts  2.1 us (1%)
    pallas_call x2, Pallas kernels, body(): call(delta_kernel, jax.ShapeDtypeStruct((3, blocks, LANES), f32), count=6...  51.9 us
    ppermute x6, starting transfers between devices, padded_2(): lax.ppermute(lax.slice_in_dim(block, block.shape[dim] - width, None, axis...  23.8 us
    pallas_call x2, Pallas kernels, body(): call(update_kernel, (jax.ShapeDtypeStruct(disp.shape, f32), jax.ShapeDtyp...  18.3 us
    pallas_call x1, Pallas kernels, body(): call(eigen_kernel, jax.ShapeDtypeStruct((blocks, LANES), f32), count=6, s...  16.1 us
    all_gather x1, blocking collectives, body(): gathered = lax.all_gather(state, 'gy', axis=3, tiled=True)  15.8 us
    ppermute x3, starting transfers between devices, neighbours(): lax.ppermute(block, axis, forward)  10.8 us
    ppermute x6, starting transfers between devices, padded_2(): lax.ppermute(lax.slice_in_dim(block, 0, width, axis=dim), axis, backward)  9.64 us
    ppermute x6, waiting for transfers between devices, padded_2(): lax.ppermute(lax.slice_in_dim(block, 0, width, axis=dim), axis, backward)  8.1 us
  transfers between devices with their start and end apart: 18, of which 10 were waited for; matrix products, arithmetic and copies ran while one was open for 0% of the time, Pallas kernels for 12%

profile of v2, /device:TPU:1, one launch (start us, length us, event | category | flops | bytes accessed | tf_op | source)
XLA Modules:
  0.0 181.5 jit_solution(11022250259389429158)
XLA Ops:
  0.6 1.0 fusion.33
  1.6 4.5 %collective-permute-start = (f32[2,8,1,256]{3,2,1,0:T(1,128)S(1)}, f32[2,8,1,256]{3,2,1,0:T(1,128)S(1)}, u32[]{:S(2)}, u32[]{:S(2)}) collective-permute-start(f32[2,8,1,256]{3,2,1,0:T(1,128)S(1)} %get-tuple-element.21), channel_id=1, source_target_pairs={{0,4},{4,8},{8,12},{1,5},{5,9},{9,13},{2,6},{6,10},{10,14},{3,7},{... | collective-permute-start | bytes 49160 | tf_op jit(solution)/shard_map/ppermute | solution.py:21
  6.2 1.9 %collective-permute-start.1 = (f32[2,8,1,256]{3,2,1,0:T(1,128)S(1)}, f32[2,8,1,256]{3,2,1,0:T(1,128)S(1)}, u32[]{:S(2)}, u32[]{:S(2)}) collective-permute-start(f32[2,8,1,256]{3,2,1,0:T(1,128)S(1)} %get-tuple-element.22), channel_id=1, source_target_pairs={{4,0},{8,4},{12,8},{5,1},{9,5},{13,9},{6,2},{10,6},{14,10},{7,3},{... | collective-permute-start | bytes 49160 | tf_op jit(solution)/shard_map/ppermute | solution.py:24
  8.1 0.0 collective-permute-done
  8.1 3.1 %collective-permute-done.1 = f32[2,8,1,256]{3,2,1,0:T(1,128)S(1)} collective-permute-done((f32[2,8,1,256]{3,2,1,0:T(1,128)S(1)}, f32[2,8,1,256]{3,2,1,0:T(1,128)S(1)}, u32[]{:S(2)}, u32[]{:S(2)}) %collective-permute-start.1) | collective-permute-done | bytes 16416 | tf_op jit(solution)/shard_map/ppermute | solution.py:24
  11.2 1.0 pad_maximum_fusion
  12.2 0.0 copy-start.10
  12.2 0.1 fusion.30
  12.3 1.3 collective-permute-start.3
  13.6 0.0 copy-start.11
  13.6 4.1 %collective-permute-start.2 = (f32[2,8,10,1]{3,2,1,0:T(8,128)S(1)}, f32[2,8,10,1]{3,2,1,0:T(8,128)S(1)}, u32[]{:S(2)}, u32[]{:S(2)}) collective-permute-start(f32[2,8,10,1]{3,2,1,0:T(8,128)S(1)} %get-tuple-element.16), channel_id=1, source_target_pairs={{0,1},{1,2},{2,3},{4,5},{5,6},{6,7},{8,9},{9,10},{10,11},{12,13},{... | collective-permute-start | bytes 1928 | tf_op jit(solution)/shard_map/ppermute | solution.py:21
  17.8 0.3 collective-permute-done.3
  18.0 1.8 collective-permute-done.2
  19.8 0.3 select_maximum_fusion.8
  20.1 0.3 fusion.2
  20.5 2.9 %collective-permute-start.4 = (f32[2,8,1,256]{3,2,1,0:T(1,128)S(1)}, f32[2,8,1,256]{3,2,1,0:T(1,128)S(1)}, u32[]{:S(2)}, u32[]{:S(2)}) collective-permute-start(f32[2,8,1,256]{3,2,1,0:T(1,128)S(1)} %get-tuple-element.19), channel_id=1, source_target_pairs={{0,4},{4,8},{8,12},{1,5},{5,9},{9,13},{2,6},{6,10},{10,14},{3,7},{... | collective-permute-start | bytes 49160 | tf_op jit(solution)/shard_map/ppermute | solution.py:21
  23.4 1.9 %collective-permute-start.5 = (f32[2,8,1,256]{3,2,1,0:T(1,128)S(1)}, f32[2,8,1,256]{3,2,1,0:T(1,128)S(1)}, u32[]{:S(2)}, u32[]{:S(2)}) collective-permute-start(f32[2,8,1,256]{3,2,1,0:T(1,128)S(1)} %get-tuple-element.20), channel_id=1, source_target_pairs={{4,0},{8,4},{12,8},{5,1},{9,5},{13,9},{6,2},{10,6},{14,10},{7,3},{... | collective-permute-start | bytes 49160 | tf_op jit(solution)/shard_map/ppermute | solution.py:24
  25.3 0.0 collective-permute-done.4
  25.3 3.1 %collective-permute-done.5 = f32[2,8,1,256]{3,2,1,0:T(1,128)S(1)} collective-permute-done((f32[2,8,1,256]{3,2,1,0:T(1,128)S(1)}, f32[2,8,1,256]{3,2,1,0:T(1,128)S(1)}, u32[]{:S(2)}, u32[]{:S(2)}) %collective-permute-start.5) | collective-permute-done | bytes 16416 | tf_op jit(solution)/shard_map/ppermute | solution.py:24
  28.5 0.1 fusion.29
  28.6 1.3 collective-permute-start.7
  29.9 4.7 %collective-permute-start.6 = (f32[2,8,10,1]{3,2,1,0:T(8,128)S(1)}, f32[2,8,10,1]{3,2,1,0:T(8,128)S(1)}, u32[]{:S(2)}, u32[]{:S(2)}) collective-permute-start(f32[2,8,10,1]{3,2,1,0:T(8,128)S(1)} %get-tuple-element.14), channel_id=1, source_target_pairs={{0,1},{1,2},{2,3},{4,5},{5,6},{6,7},{8,9},{9,10},{10,11},{12,13},{... | collective-permute-start | bytes 1928 | tf_op jit(solution)/shard_map/ppermute | solution.py:21
  34.6 0.4 collective-permute-done.7
  35.0 1.5 collective-permute-done.6
  36.5 0.3 select_maximum_fusion.4
  36.9 0.0 copy-start.3
  36.9 0.3 fusion.4
  37.2 2.8 %collective-permute-start.8 = (f32[2,8,1,256]{3,2,1,0:T(1,128)S(1)}, f32[2,8,1,256]{3,2,1,0:T(1,128)S(1)}, u32[]{:S(2)}, u32[]{:S(2)}) collective-permute-start(f32[2,8,1,256]{3,2,1,0:T(1,128)S(1)} %get-tuple-element.17), channel_id=1, source_target_pairs={{0,4},{4,8},{8,12},{1,5},{5,9},{9,13},{2,6},{6,10},{10,14},{3,7},{... | collective-permute-start | bytes 49160 | tf_op jit(solution)/shard_map/ppermute | solution.py:21
  40.0 1.9 %collective-permute-start.9 = (f32[2,8,1,256]{3,2,1,0:T(1,128)S(1)}, f32[2,8,1,256]{3,2,1,0:T(1,128)S(1)}, u32[]{:S(2)}, u32[]{:S(2)}) collective-permute-start(f32[2,8,1,256]{3,2,1,0:T(1,128)S(1)} %get-tuple-element.18), channel_id=1, source_target_pairs={{4,0},{8,4},{12,8},{5,1},{9,5},{13,9},{6,2},{10,6},{14,10},{7,3},{... | collective-permute-start | bytes 49160 | tf_op jit(solution)/shard_map/ppermute | solution.py:24
  41.9 1.9 %collective-permute-start.13 = (f32[6,8192]{1,0:T(8,128)S(1)}, f32[6,8192]{1,0:T(8,128)S(1)}, u32[]{:S(2)}, u32[]{:S(2)}) collective-permute-start(f32[6,8192]{1,0:T(8,128)S(1)} %copy-done.3), channel_id=1, source_target_pairs={{4,0},{8,4},{12,8},{5,1},{9,5},{13,9},{6,2},{10,6},{14,10},{7,3},{... | collective-permute-start | bytes 589832 | tf_op jit(solution)/shard_map/ppermute | solution.py:33
  43.9 0.0 collective-permute-done.8
  43.9 1.2 collective-permute-done.9
  45.1 0.1 fusion.28
  45.2 1.3 collective-permute-start.11
  46.5 4.7 %collective-permute-start.10 = (f32[2,8,10,1]{3,2,1,0:T(8,128)S(1)}, f32[2,8,10,1]{3,2,1,0:T(8,128)S(1)}, u32[]{:S(2)}, u32[]{:S(2)}) collective-permute-start(f32[2,8,10,1]{3,2,1,0:T(8,128)S(1)} %get-tuple-element.12), channel_id=1, source_target_pairs={{0,1},{1,2},{2,3},{4,5},{5,6},{6,7},{8,9},{9,10},{10,11},{12,13},{... | collective-permute-start | bytes 1928 | tf_op jit(solution)/shard_map/ppermute | solution.py:21
  51.2 2.8 %collective-permute-start.12 = (f32[6,8192]{1,0:T(8,128)S(1)}, f32[6,8192]{1,0:T(8,128)S(1)}, u32[]{:S(2)}, u32[]{:S(2)}) collective-permute-start(f32[6,8192]{1,0:T(8,128)S(1)} %copy-done.3), channel_id=1, source_target_pairs={{0,4},{4,8},{8,12},{1,5},{5,9},{9,13},{2,6},{6,10},{10,14},{3,7},{... | collective-permute-start | bytes 589832 | tf_op jit(solution)/shard_map/ppermute | solution.py:33
  54.0 0.0 collective-permute-done.11
  54.0 0.0 collective-permute-done.10
  54.0 0.3 select_maximum_fusion
  54.3 0.3 fusion.6
  54.6 0.0 copy-start.12
  54.6 15.8 %all_gather.3 = f32[2,8,8,1024]{3,2,1,0:T(8,128)S(1)} all-gather(f32[2,8,8,256]{3,2,1,0:T(8,128)S(1)} %fusion.6), channel_id=1, replica_groups=mesh['groups'=2,'gx'=4,'gy'=4] {'gy'}, dimensions={3}, use_global_device_ids=true | all-gather | bytes 655360 | tf_op jit(solution)/shard_map/all_gather | solution.py:281
  70.5 0.0 copy-start.4
  70.5 0.0 copy-start.8
  70.5 0.0 copy-start
  70.6 0.7 copy-done.9
  71.2 6.3 %shard_map.149.own_f = f32[2,64,128]{2,1,0:T(8,128)S(1)} custom-call(f32[2,128,128]{2,1,0:T(8,128)S(1)} %reshape.20.slab_ref, s32[64,128]{1,0:T(8,128)S(1)} %bitcast.13), custom_call_target="tpu_custom_call" | custom-call | tf_op jit(solution)/shard_map/pallas_call | solution.py:291
  77.5 2.9 %collective-permute-start.15 = (f32[2,64,128]{2,1,0:T(8,128)S(1)}, f32[2,64,128]{2,1,0:T(8,128)S(1)}, u32[]{:S(2)}, u32[]{:S(2)}) collective-permute-start(f32[2,64,128]{2,1,0:T(8,128)S(1)} %shard_map.149.own_f), channel_id=1, source_target_pairs={{4,0},{8,4},{12,8},{5,1},{9,5},{13,9},{6,2},{10,6},{14,10},{7,3},{... | collective-permute-start | bytes 196616 | tf_op jit(solution)/shard_map/ppermute | solution.py:33
  80.5 3.8 %collective-permute-start.14 = (f32[2,64,128]{2,1,0:T(8,128)S(1)}, f32[2,64,128]{2,1,0:T(8,128)S(1)}, u32[]{:S(2)}, u32[]{:S(2)}) collective-permute-start(f32[2,64,128]{2,1,0:T(8,128)S(1)} %shard_map.149.own_f), channel_id=1, source_target_pairs={{0,4},{4,8},{8,12},{1,5},{5,9},{9,13},{2,6},{6,10},{10,14},{3,7},{... | collective-permute-start | bytes 196616 | tf_op jit(solution)/shard_map/ppermute | solution.py:33
  84.9 0.0 collective-permute-done.15.next_f
  84.9 0.7 collective-permute-done.14.prev_f
  85.6 16.1 %shard_map.150.eig_ref = f32[128,128]{1,0:T(8,128)S(1)} custom-call(f32[2,64,128]{2,1,0:T(8,128)S(1)} %shard_map.149.own_f, f32[2,64,128]{2,1,0:T(8,128)S(1)} %collective-permute-done.14.prev_f, f32[2,64,128]{2,1,0:T(8,128)S(1)} %collective-permute-done.15.next_f, s32[128,128]{1,0:T(8,128)S(1)} %bitcast.5, s32[128,128]{1,0:T(8,128)S(1)} %bitcast.10, ...), custom_call_target="tpu_custom_call" | custom-call | tf_op jit(solution)/shard_map/pallas_call | solution.py:295
  101.7 0.0 copy-start.5
  101.7 0.0 copy-start.6
  101.8 0.0 copy-start.7
  101.8 0.0 collective-permute-done.13.next_q
  101.8 25.9 %shard_map.148.delta_ref = f32[3,128,128]{2,1,0:T(8,128)S(1)} custom-call(f32[6,8192]{1,0:T(8,128)S(1)} %copy-done.3, f32[6,8192]{1,0:T(8,128)S(1)} %collective-permute-done.12.prev_q, f32[6,8192]{1,0:T(8,128)S(1)} %collective-permute-done.13.next_q, s32[128,128]{1,0:T(8,128)S(1)} %bitcast.6, s32[128,128]{1,0:T(8,128)S(1)} %bitcast.11, f32[6,16384]{1,0:T(8,128)S(1)} %copy-done), custom_call_target="tpu_custom_call" | custom-call | tf_op jit(solution)/shard_map/pallas_call | solution.py:304
  127.8 8.7 %shard_map.151 = (f32[6,8192]{1,0:T(8,128)S(1)}, f32[6,8192]{1,0:T(8,128)S(1)}) custom-call(s32[1]{0:T(128)S(6)} %copy.16.live_ref, f32[3,128,128]{2,1,0:T(8,128)S(1)} %shard_map.148.delta_ref, f32[128,128]{1,0:T(8,128)S(1)} %shard_map.150.eig_ref, s32[128,128]{1,0:T(8,128)S(1)} %bitcast.7, f32[6,16384]{1,0:T(8,128)S(1)} %copy-done, ...), custom_call_target="tpu_custom_call" | custom-call | tf_op jit(solution)/shard_map/pallas_call | solution.py:308
  136.5 1.9 %collective-permute-start.17 = (f32[6,8192]{1,0:T(8,128)S(1)}, f32[6,8192]{1,0:T(8,128)S(1)}, u32[]{:S(2)}, u32[]{:S(2)}) collective-permute-start(f32[6,8192]{1,0:T(8,128)S(1)} %get-tuple-element.7.own_q.disp_ref), channel_id=1, source_target_pairs={{4,0},{8,4},{12,8},{5,1},{9,5},{13,9},{6,2},{10,6},{14,10},{7,3},{... | collective-permute-start | bytes 589832 | tf_op jit(solution)/shard_map/ppermute | solution.py:33
  138.5 4.3 %collective-permute-start.16 = (f32[6,8192]{1,0:T(8,128)S(1)}, f32[6,8192]{1,0:T(8,128)S(1)}, u32[]{:S(2)}, u32[]{:S(2)}) collective-permute-start(f32[6,8192]{1,0:T(8,128)S(1)} %get-tuple-element.7.own_q.disp_ref), channel_id=1, source_target_pairs={{0,4},{4,8},{8,12},{1,5},{5,9},{9,13},{2,6},{6,10},{10,14},{3,7},{... | collective-permute-start | bytes 589832 | tf_op jit(solution)/shard_map/ppermute | solution.py:33
  142.8 2.1 %collective-permute-done.17.next_q = f32[6,8192]{1,0:T(8,128)S(1)} collective-permute-done((f32[6,8192]{1,0:T(8,128)S(1)}, f32[6,8192]{1,0:T(8,128)S(1)}, u32[]{:S(2)}, u32[]{:S(2)}) %collective-permute-start.17) | collective-permute-done | bytes 196640 | tf_op jit(solution)/shard_map/ppermute | solution.py:33
  144.9 1.2 collective-permute-done.16.prev_q
  146.0 25.9 %shard_map.152.delta_ref = f32[3,128,128]{2,1,0:T(8,128)S(1)} custom-call(f32[6,8192]{1,0:T(8,128)S(1)} %get-tuple-element.7.own_q.disp_ref, f32[6,8192]{1,0:T(8,128)S(1)} %collective-permute-done.16.prev_q, f32[6,8192]{1,0:T(8,128)S(1)} %collective-permute-done.17.next_q, s32[128,128]{1,0:T(8,128)S(1)} %bitcast.8, s32[128,128]{1,0:T(8,128)S(1)} %bitcast.12, ...), custom_call_target="tpu_custom_call" | custom-call | tf_op jit(solution)/shard_map/pallas_call | solution.py:304
  172.0 9.5 %shard_map.153 = (f32[6,8192]{1,0:T(8,128)}, f32[6,8192]{1,0:T(8,128)}) custom-call(s32[1]{0:T(128)S(6)} %copy.16.live_ref, f32[3,128,128]{2,1,0:T(8,128)S(1)} %shard_map.152.delta_ref, f32[128,128]{1,0:T(8,128)S(1)} %shard_map.150.eig_ref, s32[128,128]{1,0:T(8,128)S(1)} %bitcast.9, f32[6,16384]{1,0:T(8,128)S(1)} %copy-done, f32[9,16384]{1,0:T(8,128)S(1)} %copy-done.1, ...), custom_call_target="tpu_custom_call" | custom-call | tf_op jit(solution)/shard_map/pallas_call | solution.py:308
  (22 shorter events, 0.2 us)
Async XLA Ops:
  1.6 6.5 %collective-permute-start = (f32[2,8,1,256]{3,2,1,0:T(1,128)S(1)}, f32[2,8,1,256]{3,2,1,0:T(1,128)S(1)}, u32[]{:S(2)}, u32[]{:S(2)}) collective-permute-start(f32[2,8,1,256]{3,2,1,0:T(1,128)S(1)} %get-tuple-element.21), channel_id=1, source_target_pairs={{0,4},{4,8},{8,12},{1,5},{5,9},{9,13},{2,6},{6,10},{10,14},{3,7},{... | collective-permute-start | bytes 49160 | tf_op jit(solution)/shard_map/ppermute | solution.py:21
  6.2 5.1 %collective-permute-start.1 = (f32[2,8,1,256]{3,2,1,0:T(1,128)S(1)}, f32[2,8,1,256]{3,2,1,0:T(1,128)S(1)}, u32[]{:S(2)}, u32[]{:S(2)}) collective-permute-start(f32[2,8,1,256]{3,2,1,0:T(1,128)S(1)} %get-tuple-element.22), channel_id=1, source_target_pairs={{4,0},{8,4},{12,8},{5,1},{9,5},{13,9},{6,2},{10,6},{14,10},{7,3},{... | collective-permute-start | bytes 49160 | tf_op jit(solution)/shard_map/ppermute | solution.py:24
  12.2 7.6 %copy-start.10 = (f32[2,8,8,256]{3,2,1,0:T(8,128)S(1)}, f32[2,8,8,256]{3,2,1,0:T(8,128)}, u32[]{:S(2)}) copy-start(f32[2,8,8,256]{3,2,1,0:T(8,128)} %param.13) | copy-start | bytes 393220
  12.3 5.7 %collective-permute-start.3 = (f32[2,8,10,1]{3,2,1,0:T(8,128)S(1)}, f32[2,8,10,1]{3,2,1,0:T(8,128)S(1)}, u32[]{:S(2)}, u32[]{:S(2)}) collective-permute-start(f32[2,8,10,1]{3,2,1,0:T(8,128)S(1)} %get-tuple-element.15), channel_id=1, source_target_pairs={{1,0},{2,1},{3,2},{5,4},{6,5},{7,6},{9,8},{10,9},{11,10},{13,12},{... | collective-permute-start | bytes 1928 | tf_op jit(solution)/shard_map/ppermute | solution.py:24
  13.6 6.5 %copy-start.11 = (f32[2,8,8,256]{3,2,1,0:T(8,128)S(1)}, f32[2,8,8,256]{3,2,1,0:T(8,128)}, u32[]{:S(2)}) copy-start(f32[2,8,8,256]{3,2,1,0:T(8,128)} %param.14) | copy-start | bytes 393220
  13.6 6.2 %collective-permute-start.2 = (f32[2,8,10,1]{3,2,1,0:T(8,128)S(1)}, f32[2,8,10,1]{3,2,1,0:T(8,128)S(1)}, u32[]{:S(2)}, u32[]{:S(2)}) collective-permute-start(f32[2,8,10,1]{3,2,1,0:T(8,128)S(1)} %get-tuple-element.16), channel_id=1, source_target_pairs={{0,1},{1,2},{2,3},{4,5},{5,6},{6,7},{8,9},{9,10},{10,11},{12,13},{... | collective-permute-start | bytes 1928 | tf_op jit(solution)/shard_map/ppermute | solution.py:21
  20.5 4.9 %collective-permute-start.4 = (f32[2,8,1,256]{3,2,1,0:T(1,128)S(1)}, f32[2,8,1,256]{3,2,1,0:T(1,128)S(1)}, u32[]{:S(2)}, u32[]{:S(2)}) collective-permute-start(f32[2,8,1,256]{3,2,1,0:T(1,128)S(1)} %get-tuple-element.19), channel_id=1, source_target_pairs={{0,4},{4,8},{8,12},{1,5},{5,9},{9,13},{2,6},{6,10},{10,14},{3,7},{... | collective-permute-start | bytes 49160 | tf_op jit(solution)/shard_map/ppermute | solution.py:21
  23.4 5.1 %collective-permute-start.5 = (f32[2,8,1,256]{3,2,1,0:T(1,128)S(1)}, f32[2,8,1,256]{3,2,1,0:T(1,128)S(1)}, u32[]{:S(2)}, u32[]{:S(2)}) collective-permute-start(f32[2,8,1,256]{3,2,1,0:T(1,128)S(1)} %get-tuple-element.20), channel_id=1, source_target_pairs={{4,0},{8,4},{12,8},{5,1},{9,5},{13,9},{6,2},{10,6},{14,10},{7,3},{... | collective-permute-start | bytes 49160 | tf_op jit(solution)/shard_map/ppermute | solution.py:24
  28.6 6.4 %collective-permute-start.7 = (f32[2,8,10,1]{3,2,1,0:T(8,128)S(1)}, f32[2,8,10,1]{3,2,1,0:T(8,128)S(1)}, u32[]{:S(2)}, u32[]{:S(2)}) collective-permute-start(f32[2,8,10,1]{3,2,1,0:T(8,128)S(1)} %get-tuple-element.13), channel_id=1, source_target_pairs={{1,0},{2,1},{3,2},{5,4},{6,5},{7,6},{9,8},{10,9},{11,10},{13,12},{... | collective-permute-start | bytes 1928 | tf_op jit(solution)/shard_map/ppermute | solution.py:24
  29.9 6.6 %collective-permute-start.6 = (f32[2,8,10,1]{3,2,1,0:T(8,128)S(1)}, f32[2,8,10,1]{3,2,1,0:T(8,128)S(1)}, u32[]{:S(2)}, u32[]{:S(2)}) collective-permute-start(f32[2,8,10,1]{3,2,1,0:T(8,128)S(1)} %get-tuple-element.14), channel_id=1, source_target_pairs={{0,1},{1,2},{2,3},{4,5},{5,6},{6,7},{8,9},{9,10},{10,11},{12,13},{... | collective-permute-start | bytes 1928 | tf_op jit(solution)/shard_map/ppermute | solution.py:21
  36.9 5.1 %copy-start.3 = (f32[6,8192]{1,0:T(8,128)S(1)}, f32[6,8192]{1,0:T(8,128)}, u32[]{:S(2)}) copy-start(f32[6,8192]{1,0:T(8,128)} %disp_ref.1) | copy-start | bytes 589828
  37.2 6.7 %collective-permute-start.8 = (f32[2,8,1,256]{3,2,1,0:T(1,128)S(1)}, f32[2,8,1,256]{3,2,1,0:T(1,128)S(1)}, u32[]{:S(2)}, u32[]{:S(2)}) collective-permute-start(f32[2,8,1,256]{3,2,1,0:T(1,128)S(1)} %get-tuple-element.17), channel_id=1, source_target_pairs={{0,4},{4,8},{8,12},{1,5},{5,9},{9,13},{2,6},{6,10},{10,14},{3,7},{... | collective-permute-start | bytes 49160 | tf_op jit(solution)/shard_map/ppermute | solution.py:21
  40.0 5.1 %collective-permute-start.9 = (f32[2,8,1,256]{3,2,1,0:T(1,128)S(1)}, f32[2,8,1,256]{3,2,1,0:T(1,128)S(1)}, u32[]{:S(2)}, u32[]{:S(2)}) collective-permute-start(f32[2,8,1,256]{3,2,1,0:T(1,128)S(1)} %get-tuple-element.18), channel_id=1, source_target_pairs={{4,0},{8,4},{12,8},{5,1},{9,5},{13,9},{6,2},{10,6},{14,10},{7,3},{... | collective-permute-start | bytes 49160 | tf_op jit(solution)/shard_map/ppermute | solution.py:24
  41.9 59.8 %collective-permute-start.13 = (f32[6,8192]{1,0:T(8,128)S(1)}, f32[6,8192]{1,0:T(8,128)S(1)}, u32[]{:S(2)}, u32[]{:S(2)}) collective-permute-start(f32[6,8192]{1,0:T(8,128)S(1)} %copy-done.3), channel_id=1, source_target_pairs={{4,0},{8,4},{12,8},{5,1},{9,5},{13,9},{6,2},{10,6},{14,10},{7,3},{... | collective-permute-start | bytes 589832 | tf_op jit(solution)/shard_map/ppermute | solution.py:33
  45.2 8.8 %collective-permute-start.11 = (f32[2,8,10,1]{3,2,1,0:T(8,128)S(1)}, f32[2,8,10,1]{3,2,1,0:T(8,128)S(1)}, u32[]{:S(2)}, u32[]{:S(2)}) collective-permute-start(f32[2,8,10,1]{3,2,1,0:T(8,128)S(1)} %get-tuple-element.11), channel_id=1, source_target_pairs={{1,0},{2,1},{3,2},{5,4},{6,5},{7,6},{9,8},{10,9},{11,10},{13,12},{... | collective-permute-start | bytes 1928 | tf_op jit(solution)/shard_map/ppermute | solution.py:24
  46.5 7.5 %collective-permute-start.10 = (f32[2,8,10,1]{3,2,1,0:T(8,128)S(1)}, f32[2,8,10,1]{3,2,1,0:T(8,128)S(1)}, u32[]{:S(2)}, u32[]{:S(2)}) collective-permute-start(f32[2,8,10,1]{3,2,1,0:T(8,128)S(1)} %get-tuple-element.12), channel_id=1, source_target_pairs={{0,1},{1,2},{2,3},{4,5},{5,6},{6,7},{8,9},{9,10},{10,11},{12,13},{... | collective-permute-start | bytes 1928 | tf_op jit(solution)/shard_map/ppermute | solution.py:21
  51.2 50.6 %collective-permute-start.12 = (f32[6,8192]{1,0:T(8,128)S(1)}, f32[6,8192]{1,0:T(8,128)S(1)}, u32[]{:S(2)}, u32[]{:S(2)}) collective-permute-start(f32[6,8192]{1,0:T(8,128)S(1)} %copy-done.3), channel_id=1, source_target_pairs={{0,4},{4,8},{8,12},{1,5},{5,9},{9,13},{2,6},{6,10},{10,14},{3,7},{... | collective-permute-start | bytes 589832 | tf_op jit(solution)/shard_map/ppermute | solution.py:33
  54.6 15.8 %copy-start.12 = (f32[2,8,8,256]{3,2,1,0:T(8,128)}, f32[2,8,8,256]{3,2,1,0:T(8,128)S(1)}, u32[]{:S(2)}) copy-start(f32[2,8,8,256]{3,2,1,0:T(8,128)S(1)} %fusion.6) | copy-start | bytes 393220
  70.5 0.8 copy-start.9
  70.5 15.1 %copy-start.2 = (s32[16384]{0:T(1024)S(1)}, s32[16384]{0:T(1024)}, u32[]{:S(2)}) copy-start(s32[16384]{0:T(1024)} %param.19) | copy-start | bytes 196612
  70.5 15.1 %copy-start.4 = (s32[16384]{0:T(1024)S(1)}, s32[16384]{0:T(1024)}, u32[]{:S(2)}) copy-start(s32[16384]{0:T(1024)} %param.20) | copy-start | bytes 196612
  70.5 15.1 %copy-start.8 = (f32[2,16384]{1,0:T(2,128)S(1)}, f32[2,16384]{1,0:T(2,128)}, u32[]{:S(2)}) copy-start(f32[2,16384]{1,0:T(2,128)} %eigen_ref.1) | copy-start | bytes 393220
  70.5 31.3 %copy-start = (f32[6,16384]{1,0:T(8,128)S(1)}, f32[6,16384]{1,0:T(8,128)}, u32[]{:S(2)}) copy-start(f32[6,16384]{1,0:T(8,128)} %arms_ref.7) | copy-start | bytes 1179652
  77.5 7.4 %collective-permute-start.15 = (f32[2,64,128]{2,1,0:T(8,128)S(1)}, f32[2,64,128]{2,1,0:T(8,128)S(1)}, u32[]{:S(2)}, u32[]{:S(2)}) collective-permute-start(f32[2,64,128]{2,1,0:T(8,128)S(1)} %shard_map.149.own_f), channel_id=1, source_target_pairs={{4,0},{8,4},{12,8},{5,1},{9,5},{13,9},{6,2},{10,6},{14,10},{7,3},{... | collective-permute-start | bytes 196616 | tf_op jit(solution)/shard_map/ppermute | solution.py:33
  80.5 5.1 %collective-permute-start.14 = (f32[2,64,128]{2,1,0:T(8,128)S(1)}, f32[2,64,128]{2,1,0:T(8,128)S(1)}, u32[]{:S(2)}, u32[]{:S(2)}) collective-permute-start(f32[2,64,128]{2,1,0:T(8,128)S(1)} %shard_map.149.own_f), channel_id=1, source_target_pairs={{0,4},{4,8},{8,12},{1,5},{5,9},{9,13},{2,6},{6,10},{10,14},{3,7},{... | collective-permute-start | bytes 196616 | tf_op jit(solution)/shard_map/ppermute | solution.py:33
  85.6 42.2 %copy-start.1 = (f32[9,16384]{1,0:T(8,128)S(1)}, f32[9,16384]{1,0:T(8,128)}, u32[]{:S(2)}) copy-start(f32[9,16384]{1,0:T(8,128)} %frame_ref.3) | copy-start | bytes 1769476
  101.7 26.0 %copy-start.5 = (f32[2,16384]{1,0:T(2,128)S(1)}, f32[2,16384]{1,0:T(2,128)}, u32[]{:S(2)}) copy-start(f32[2,16384]{1,0:T(2,128)} %stiff_ref.3) | copy-start | bytes 393220
  101.7 26.0 %copy-start.6 = (f32[2,8192]{1,0:T(2,128)S(1)}, f32[2,8192]{1,0:T(2,128)}, u32[]{:S(2)}) copy-start(f32[2,8192]{1,0:T(2,128)} %inertia_ref.3) | copy-start | bytes 196612
  101.8 26.0 %copy-start.7 = (f32[6,8192]{1,0:T(8,128)S(1)}, f32[6,8192]{1,0:T(8,128)}, u32[]{:S(2)}) copy-start(f32[6,8192]{1,0:T(8,128)} %vel_ref.1) | copy-start | bytes 589828
  136.5 8.3 %collective-permute-start.17 = (f32[6,8192]{1,0:T(8,128)S(1)}, f32[6,8192]{1,0:T(8,128)S(1)}, u32[]{:S(2)}, u32[]{:S(2)}) collective-permute-start(f32[6,8192]{1,0:T(8,128)S(1)} %get-tuple-element.7.own_q.disp_ref), channel_id=1, source_target_pairs={{4,0},{8,4},{12,8},{5,1},{9,5},{13,9},{6,2},{10,6},{14,10},{7,3},{... | collective-permute-start | bytes 589832 | tf_op jit(solution)/shard_map/ppermute | solution.py:33
  138.5 7.6 %collective-permute-start.16 = (f32[6,8192]{1,0:T(8,128)S(1)}, f32[6,8192]{1,0:T(8,128)S(1)}, u32[]{:S(2)}, u32[]{:S(2)}) collective-permute-start(f32[6,8192]{1,0:T(8,128)S(1)} %get-tuple-element.7.own_q.disp_ref), channel_id=1, source_target_pairs={{0,4},{4,8},{8,12},{1,5},{5,9},{9,13},{2,6},{6,10},{10,14},{3,7},{... | collective-permute-start | bytes 589832 | tf_op jit(solution)/shard_map/ppermute | solution.py:33

commit v3 on v2

--- a/solution.py
+++ b/solution.py
@@ -13,19 +13,6 @@
 VMEM_LIMIT = 48 * 1024 * 1024
 
 
-def padded_2(block, sides, width):
-    for axis, dim in sides:
-        count = lax.axis_size(axis)
-        forward = [(i, i + 1) for i in range(count - 1)]
-        backward = [(target, source) for source, target in forward]
-        low = lax.ppermute(
-            lax.slice_in_dim(block, block.shape[dim] - width, None, axis=dim), axis, forward
-        )
-        high = lax.ppermute(lax.slice_in_dim(block, 0, width, axis=dim), axis, backward)
-        block = jnp.concatenate([low, block, high], axis=dim)
-    return block
-
-
 def neighbours(block, axis):
     count = lax.axis_size(axis)
     forward = [(i, i + 1) for i in range(count - 1)]
@@ -33,31 +20,155 @@
     return lax.ppermute(block, axis, forward), lax.ppermute(block, axis, backward)
 
 
-def advance_plan(extended, rates):
-    padded = jnp.pad(extended, ((0, 0), (1, 1), (0, 0), (0, 0)))
-    center = padded[:, 1:-1, 1:-1, 1:-1]
-    laplace = padded[:, 2:, 1:-1, 1:-1] + padded[:, :-2, 1:-1, 1:-1]
-    laplace = laplace + padded[:, 1:-1, 2:, 1:-1] + padded[:, 1:-1, :-2, 1:-1]
-    laplace = laplace + padded[:, 1:-1, 1:-1, 2:] + padded[:, 1:-1, 1:-1, :-2] - 6.0 * center
-    return center + rates * laplace + couple_rate * (center[::-1] - center)
+def flow_kernel(cell_ref, rate_ref, disp_ref, state_out, slab_out, prev_out, next_out,
+                held, crest_edge, crest_halo, plan_halo,
+                crest_send, crest_recv, plan_send, plan_recv, disp_send, disp_recv,
+                slab_send, slab_recv):
+    x, y = lax.axis_index("gx"), lax.axis_index("gy")
+    nx, ny = lax.axis_size("gx"), lax.axis_size("gy")
+    rows, layers, crest, thick = cell_ref.shape
+    slab = layers // ny
+    has_lo, has_hi = (x > 0, y > 0), (x < nx - 1, y < ny - 1)
+
+    barrier = pltpu.get_barrier_semaphore()
+
+    def greet(axis, target):
+        pl.semaphore_signal(barrier, inc=1, device_id={axis: target},
+                            device_id_type=pl.DeviceIdType.MESH)
+
+    @pl.when(has_lo[0])
+    def _():
+        greet("gx", x - 1)
+
+    @pl.when(has_hi[0])
+    def _():
+        greet("gx", x + 1)
+
+    for o in range(1, ny):
+        greet("gy", lax.rem(y + o, ny))
+    greeted = jnp.where(has_lo[0], 1, 0) + jnp.where(has_hi[0], 1, 0) + (ny - 1)
+    pl.semaphore_wait(barrier, greeted)
+
+    def remote(src, dst, send, recv, axis, target):
+        return pltpu.make_async_remote_copy(
+            src_ref=src, dst_ref=dst, send_sem=send, recv_sem=recv,
+            device_id={axis: target}, device_id_type=pl.DeviceIdType.MESH)
+
+    def both_ways(axis, lo_src, hi_src, lo_dst, hi_dst, send, recv):
+        at, i = (x, 0) if axis == "gx" else (y, 1)
+        down = remote(lo_src, hi_dst, send.at[0], recv.at[0], axis, at - 1)
+        up = remote(hi_src, lo_dst, send.at[1], recv.at[1], axis, at + 1)
+        return has_lo[i], has_hi[i], down, up, lo_dst, hi_dst
+
+    def start(pair):
+        lo, hi, down, up, lo_dst, hi_dst = pair
+
+        @pl.when(lo)
+        def _():
+            down.start()
+
+        @pl.when(hi)
+        def _():
+            up.start()
+
+        @pl.when(jnp.logical_not(lo))
+        def _():
+            lo_dst[...] = jnp.zeros_like(lo_dst)
+
+        @pl.when(jnp.logical_not(hi))
+        def _():
+            hi_dst[...] = jnp.zeros_like(hi_dst)
+
+    def finish(pair):
+        lo, hi, down, up, _, _ = pair
+
+        @pl.when(lo)
+        def _():
+            down.wait_send()
+            up.wait_recv()
+
+        @pl.when(hi)
+        def _():
+            up.wait_send()
+            down.wait_recv()
+
+    states = [cell_ref, held.at[0], held.at[1], state_out]
+    lane = lax.broadcasted_iota(jnp.int32, (crest, thick), 1)
+    line = lax.broadcasted_iota(jnp.int32, (crest, thick), 0)
+    whole = (crest, thick)
+    disp_pair = both_ways("gx", disp_ref, disp_ref, prev_out, next_out, disp_send, disp_recv)
+    for step in range(3):
+        now, later = states[step], states[step + 1]
+        for r in range(rows):
+            for l in range(layers):
+                crest_edge[step, 0, r, l:l + 1, :] = now[r, l, 0:1, :]
+                crest_edge[step, 1, r, l:l + 1, :] = now[r, l, crest - 1:crest, :]
+        crest_pair = both_ways("gx", crest_edge.at[step, 0], crest_edge.at[step, 1],
+                               crest_halo.at[step, 0], crest_halo.at[step, 1],
+                               crest_send.at[step], crest_recv.at[step])
+        plan_pair = both_ways("gy", now.at[:, :, :, 0:LANES], now.at[:, :, :, thick - LANES:thick],
+                              plan_halo.at[step, 0], plan_halo.at[step, 1],
+                              plan_send.at[step], plan_recv.at[step])
+        start(plan_pair)
+        start(crest_pair)
+        if step == 0:
+            start(disp_pair)
+        finish(plan_pair)
+        finish(crest_pair)
+        for l in range(layers):
+            center = [now[r, l] for r in range(rows)]
+            for r in range(rows):
+                c = center[r]
+                none = jnp.zeros_like(c)
+                lap = (now[r, l + 1] if l + 1 < layers else none) + (now[r, l - 1] if l > 0 else none)
+                lap += jnp.where(line == crest - 1,
+                                 jnp.broadcast_to(crest_halo[step, 1, r, l:l + 1, :], whole),
+                                 pltpu.roll(c, crest - 1, 0))
+                lap += jnp.where(line == 0,
+                                 jnp.broadcast_to(crest_halo[step, 0, r, l:l + 1, :], whole),
+                                 pltpu.roll(c, 1, 0))
+                hi_col = plan_halo[step, 1, r, l][:, 0:1]
+                lo_col = plan_halo[step, 0, r, l][:, LANES - 1:LANES]
+                lap += jnp.where(lane == thick - 1, jnp.broadcast_to(hi_col, whole),
+                                 pltpu.roll(c, thick - 1, 1))
+                lap += jnp.where(lane == 0, jnp.broadcast_to(lo_col, whole), pltpu.roll(c, 1, 1))
+                lap -= 6.0 * c
+                later[r, l] = c + rate_ref[r, l] * lap + couple_rate * (center[1 - r] - c)
+
+    copies = []
+    for o in range(1, ny):
+        target = lax.rem(y + o, ny)
+        copies.append(remote(state_out.at[:, pl.ds(target * slab, slab)], slab_out.at[y],
+                             slab_send.at[o - 1], slab_recv.at[o - 1], "gy", target))
+    for copy in copies:
+        copy.start()
+    slab_out[y] = state_out[:, pl.ds(y * slab, slab)]
+    for copy in copies:
+        copy.wait()
+    finish(disp_pair)
 
 
 WIDE = 256
 
 
-def fill_table(table, staged, sources, rows):
-    total = staged.shape[0] // rows
+def stage_rows(staged, sources, first, total):
     base = 0
     for ref in sources:
+        rows = ref.shape[0]
         if len(ref.shape) == 3:
             count = ref.shape[1]
             for r in range(rows):
-                staged[r * total + base:r * total + base + count, :] = ref[r]
+                at = (first + r) * total + base
+                staged[at:at + count, :] = ref[r]
         else:
             count = ref.shape[1] // LANES
             for h in range(count):
-                staged[pl.ds(base + h, rows, stride=total), :] = ref[:, h * LANES:(h + 1) * LANES]
+                staged[pl.ds(first * total + base + h, rows, stride=total), :] = (
+                    ref[:, h * LANES:(h + 1) * LANES])
         base += count
+
+
+def split_table(table, staged):
     value = staged[...]
     top = value.astype(jnp.bfloat16)
     table[:, 0:LANES] = top
@@ -118,7 +229,17 @@
 
 
 def host_kernel(slab_ref, host_ref, out_ref, staged, table, found):
-    fill_table(table, staged, [slab_ref], 2)
+    sources, _, layers, crest, thick = slab_ref.shape
+    pieces = thick // LANES
+    line = sources * pieces
+    for j in range(sources):
+        for r in range(2):
+            for l in range(layers):
+                for p in range(pieces):
+                    at = ((r * layers + l) * crest) * line + j * pieces + p
+                    staged[pl.ds(at, crest, stride=line), :] = (
+                        slab_ref[j, r, l, :, p * LANES:(p + 1) * LANES])
+    split_table(table, staged)
 
     def chunk(g, carry):
         look(table, 2, index_of(host_ref, g), found, pl.multiple_of(g * 8 * (WIDE // LANES), 8))
@@ -137,10 +258,16 @@
     return [stage[pl.ds(m, 8 * GROUP, stride=rows), :] for m in range(rows)]
 
 
-def find_both(rows, own_ref, other_ref, own_q, prev_q, next_q, scratch):
+def find_both(own_ref, other_ref, owners, windows, scratch):
     staged_a, table_a, found_a, staged_b, table_b, found_b = scratch
-    fill_table(table_a, staged_a, [own_q], rows)
-    fill_table(table_b, staged_b, [prev_q, own_q, next_q], rows)
+    rows = sum(ref.shape[0] for ref in owners)
+    first = 0
+    for ref, three in zip(owners, windows):
+        stage_rows(staged_a, [ref], first, staged_a.shape[0] // rows)
+        stage_rows(staged_b, three, first, staged_b.shape[0] // rows)
+        first += ref.shape[0]
+    split_table(table_a, staged_a)
+    split_table(table_b, staged_b)
 
     def chunk(g, carry):
         at = pl.multiple_of(g * 8 * (WIDE // LANES), 8)
@@ -152,33 +279,39 @@
     return found_a, found_b
 
 
-def eigen_kernel(own_f, prev_f, next_f, own_ref, other_ref, eigen_ref, out_ref, stage, *scratch):
-    found_a, found_b = find_both(2, own_ref, other_ref, own_f, prev_f, next_f, scratch)
+def delta_at(found_a, found_b, arms_ref, out_ref, stage, at):
+    a = [gathered_row(found_a, r, at, 8 * GROUP) for r in range(6)]
+    b = [gathered_row(found_b, r, at, 8 * GROUP) for r in range(6)]
+    arms = unpack(arms_ref, at, 6, stage)
+    turn_a = cross(a[3:6], arms[0:3])
+    turn_b = cross(b[3:6], arms[3:6])
+    for m in range(3):
+        out_ref[m, pl.ds(at, 8 * GROUP), :] = (b[m] + turn_b[m]) - (a[m] + turn_a[m])
+
+
+def first_kernel(own_q, prev_q, next_q, own_f, prev_f, next_f, own_ref, other_ref, arms_ref,
+                 eigen_ref, out_ref, eig_ref, stage, *scratch):
+    found_a, found_b = find_both(own_ref, other_ref, [own_q, own_f],
+                                 [[prev_q, own_q, next_q], [prev_f, own_f, next_f]], scratch)
 
     def chunk(g, carry):
         at = pl.multiple_of(g * 8 * GROUP, 8 * GROUP)
+        delta_at(found_a, found_b, arms_ref, out_ref, stage, at)
         eig = unpack(eigen_ref, at, 2, stage)
         pore, heat = [
             gathered_row(found_a, r, at, 8 * GROUP) + gathered_row(found_b, r, at, 8 * GROUP)
-            for r in range(2)]
-        out_ref[pl.ds(at, 8 * GROUP), :] = 0.5 * (eig[0] * heat + eig[1] * pore)
+            for r in (6, 7)]
+        eig_ref[pl.ds(at, 8 * GROUP), :] = 0.5 * (eig[0] * heat + eig[1] * pore)
         return carry
 
     lax.fori_loop(0, own_ref.shape[0] // (8 * GROUP), chunk, 0)
 
 
 def delta_kernel(own_q, prev_q, next_q, own_ref, other_ref, arms_ref, out_ref, stage, *scratch):
-    found_a, found_b = find_both(6, own_ref, other_ref, own_q, prev_q, next_q, scratch)
+    found_a, found_b = find_both(own_ref, other_ref, [own_q], [[prev_q, own_q, next_q]], scratch)
 
     def chunk(g, carry):
-        at = pl.multiple_of(g * 8 * GROUP, 8 * GROUP)
-        a = [gathered_row(found_a, r, at, 8 * GROUP) for r in range(6)]
-        b = [gathered_row(found_b, r, at, 8 * GROUP) for r in range(6)]
-        arms = unpack(arms_ref, at, 6, stage)
-        turn_a = cross(a[3:6], arms[0:3])
-        turn_b = cross(b[3:6], arms[3:6])
-        for m in range(3):
-            out_ref[m, pl.ds(at, 8 * GROUP), :] = (b[m] + turn_b[m]) - (a[m] + turn_a[m])
+        delta_at(found_a, found_b, arms_ref, out_ref, stage, pl.multiple_of(g * 8 * GROUP, 8 * GROUP))
         return carry
 
     lax.fori_loop(0, own_ref.shape[0] // (8 * GROUP), chunk, 0)
@@ -272,15 +405,28 @@
     other = facet_other.reshape(blocks, LANES)
     per = 8 * GROUP
 
-    state = cell_start
-    for substep in range(3):
-        extended = padded_2(state, (("gx", 2), ("gy", 3)), 1)
-        state = advance_plan(extended, diffusivity)
-    layers = state.shape[1]
-    slab_rows = layers // lax.axis_size("gy")
-    gathered = lax.all_gather(state, "gy", axis=3, tiled=True)
-    slab = lax.dynamic_slice_in_dim(gathered, lax.axis_index("gy") * slab_rows, slab_rows, 1)
-    slab = slab.reshape(2, -1, LANES)
+    ny = lax.axis_size("gy")
+    rows, layers, crest, thick = cell_start.shape
+    dma = pltpu.SemaphoreType.DMA
+    shape = lambda *dims: jax.ShapeDtypeStruct(dims, f32)
+    vmem = pl.BlockSpec(memory_space=pltpu.VMEM)
+    state, slab, prev_q, next_q = pl.pallas_call(
+        flow_kernel,
+        out_shape=(shape(*cell_start.shape), shape(ny, rows, layers // ny, crest, thick),
+                   shape(*disp_start.shape), shape(*disp_start.shape)),
+        in_specs=[vmem] * 3,
+        out_specs=(vmem,) * 4,
+        scratch_shapes=[
+            pltpu.VMEM((2,) + cell_start.shape, f32),
+            pltpu.VMEM((3, 2, rows, layers, thick), f32),
+            pltpu.VMEM((3, 2, rows, layers, thick), f32),
+            pltpu.VMEM((3, 2, rows, layers, crest, LANES), f32),
+            dma((3, 2)), dma((3, 2)), dma((3, 2)), dma((3, 2)), dma((2,)), dma((2,)),
+            dma((ny - 1,)), dma((ny - 1,)),
+        ],
+        compiler_params=pltpu.CompilerParams(
+            vmem_limit_bytes=VMEM_LIMIT, collective_id=0, has_side_effects=True),
+    )(cell_start, diffusivity, disp_start)
 
     def tables(rows, high, found):
         return [pltpu.VMEM((rows * high, LANES), f32),
@@ -289,22 +435,23 @@
 
     high = particles // LANES
     fields = call(host_kernel, jax.ShapeDtypeStruct((2, high, LANES), f32), count=2,
-                  scratch=tables(2, slab.shape[1], high))(
+                  scratch=tables(2, slab.size // (2 * LANES), high))(
         slab, host_cell.reshape(-1, LANES))
     prev_f, next_f = neighbours(fields, "gx")
-    eig = call(eigen_kernel, jax.ShapeDtypeStruct((blocks, LANES), f32), count=6,
-               scratch=[pltpu.VMEM((per * 2, LANES), f32)] + tables(2, high, blocks)
-               + tables(2, 3 * high, blocks))(
-        fields, prev_f, next_f, own, other, facet_eigen)
+    delta, eig = call(first_kernel, (shape(3, blocks, LANES), shape(blocks, LANES)), count=10,
+                      scratch=[pltpu.VMEM((per * 6, LANES), f32)] + tables(8, high, blocks)
+                      + tables(8, 3 * high, blocks))(
+        disp_start, prev_q, next_q, fields, prev_f, next_f, own, other, facet_arms, facet_eigen)
 
     disp, vel = disp_start, vel_start
     high_count = particles // (2 * LANES)
     for substep in range(2):
-        prev_q, next_q = neighbours(disp, "gx")
-        delta = call(delta_kernel, jax.ShapeDtypeStruct((3, blocks, LANES), f32), count=6,
-                     scratch=[pltpu.VMEM((per * 6, LANES), f32)] + tables(6, high, blocks)
-                     + tables(6, 3 * high, blocks))(
-            disp, prev_q, next_q, own, other, facet_arms)
+        if substep > 0:
+            prev_q, next_q = neighbours(disp, "gx")
+            delta = call(delta_kernel, jax.ShapeDtypeStruct((3, blocks, LANES), f32), count=6,
+                         scratch=[pltpu.VMEM((per * 6, LANES), f32)] + tables(6, high, blocks)
+                         + tables(6, 3 * high, blocks))(
+                disp, prev_q, next_q, own, other, facet_arms)
         disp, vel = call(
             update_kernel,
             (jax.ShapeDtypeStruct(disp.shape, f32), jax.ShapeDtypeStruct(vel.shape, f32)),

time: 183 us -> 127 us (0.69)
  starting transfers between devices: 51 us -> 11.8 us
  blocking collectives: 15.8 us -> 0 us
  waiting for transfers between devices: 15.4 us -> 3.95 us
  Pallas kernels: 92.6 us -> 101 us
  local copies, waits for them, and re-layouts: 2.1 us -> 7.87 us
  other arithmetic: 2.85 us -> 0 us
    pallas_call x1 -> x2, Pallas kernels: 16.1 us -> 50.7 us  [the longest x1 30.9 us: body(): call(first_kernel, (shape(3, blocks, LANES), shape(blocks, LANES)), count...]
    ppermute x12 -> x0, starting transfers between devices: 33.4 us -> none  [the longest x6 23.8 us: padded_2(): lax.ppermute(lax.slice_in_dim(block, block.shape[dim] - width, None, axis...]
    pallas_call x2 -> x1, Pallas kernels: 51.9 us -> 26 us  [body(): call(delta_kernel, jax.ShapeDtypeStruct((3, blocks, LANES), f32), count=6...]
    all_gather x1 -> x0, blocking collectives: 15.8 us -> none  [body(): gathered = lax.all_gather(state, 'gy', axis=3, tiled=True)]
    ppermute x12 -> x0, waiting for transfers between devices: 11.4 us -> none  [the longest x6 8.1 us: padded_2(): lax.ppermute(lax.slice_in_dim(block, 0, width, axis=dim), axis, backward)]
    unnamed x26 -> x31, local copies, waits for them, and re-layouts: 0.73 us -> 7.87 us
    ppermute x3 -> x2, starting transfers between devices: 10.8 us -> 7.23 us  [neighbours(): lax.ppermute(block, axis, forward)]
    ppermute x3 -> x2, starting transfers between devices: 6.76 us -> 4.52 us  [neighbours(): lax.ppermute(block, axis, backward)]
  transfers between devices with their start and end apart: 18 -> 4, of which waited for: 10 -> 3; matrix products, arithmetic and copies ran while one was open for 0% -> 0% of each run, Pallas kernels for 12% -> 0%
where the time goes in v3:
time: 127 us; the launch traced here: 126 us
  Pallas kernels  101 us (80%)
  starting transfers between devices  11.8 us (9%)
  local copies, waits for them, and re-layouts  7.87 us (6%)
  waiting for transfers between devices  3.95 us (3%)
  between operations  1.45 us (1%)
    pallas_call x1, Pallas kernels, body(): call(first_kernel, (shape(3, blocks, LANES), shape(blocks, LANES)), count...  30.9 us
    pallas_call x1, Pallas kernels, body(): call(delta_kernel, jax.ShapeDtypeStruct((3, blocks, LANES), f32), count=6...  26 us
    pallas_call x1, Pallas kernels, body(): pl.pallas_call(flow_kernel, out_shape=(shape(*cell_start.shape), shape(ny...  19.8 us
    pallas_call x2, Pallas kernels, body(): call(update_kernel, (jax.ShapeDtypeStruct(disp.shape, f32), jax.ShapeDtyp...  18.3 us
    unnamed x31, local copies, waits for them, and re-layouts  7.87 us
    ppermute x2, starting transfers between devices, neighbours(): lax.ppermute(block, axis, forward)  7.23 us
    pallas_call x1, Pallas kernels, body(): call(host_kernel, jax.ShapeDtypeStruct((2, high, LANES), f32), count=2, s...  6.32 us
    ppermute x2, starting transfers between devices, neighbours(): lax.ppermute(block, axis, backward)  4.52 us
  transfers between devices with their start and end apart: 4, of which 3 were waited for; matrix products, arithmetic and copies ran while one was open for 0% of the time, Pallas kernels for 0%

profile of v3, /device:TPU:1, one launch (start us, length us, event | category | flops | bytes accessed | tf_op | source)
XLA Modules:
  0.0 126.3 jit_solution(5348795535292937302)
XLA Ops:
  0.6 0.0 copy-start
  0.6 0.0 copy-start.2
  0.7 1.0 copy-done.2
  1.7 0.0 copy-start.12
  1.7 0.9 copy-done.12
  2.6 0.0 copy-start.13
  2.6 0.9 copy-done.13
  3.5 19.8 %shard_map.148 = (f32[2,8,8,256]{3,2,1,0:T(8,128)S(1)}, f32[4,2,2,8,256]{4,3,2,1,0:T(8,128)S(1)}, f32[6,8192]{1,0:T(8,128)S(1)}, f32[6,8192]{1,0:T(8,128)S(1)}) custom-call(f32[2,8,8,256]{3,2,1,0:T(8,128)S(1)} %copy-done.12, f32[2,8,8,256]{3,2,1,0:T(8,128)S(1)} %copy-done.13, f32[6,8192]{1,0:T(8,128)S(1)} %copy-done.2), custom_call_target="tpu_custom_call" | custom-call | tf_op jit(solution)/shard_map/pallas_call | solution.py:413
  23.2 0.0 copy-start.1
  23.2 0.0 copy-start.14
  23.2 0.8 copy-done.14
  24.1 6.3 %shard_map.149.own_f = f32[2,64,128]{2,1,0:T(8,128)S(1)} custom-call(f32[4,2,2,8,256]{4,3,2,1,0:T(8,128)S(1)} %get-tuple-element.16.slab_ref, s32[64,128]{1,0:T(8,128)S(1)} %bitcast.9), custom_call_target="tpu_custom_call" | custom-call | tf_op jit(solution)/shard_map/pallas_call | solution.py:437
  30.4 2.6 %collective-permute-start.1 = (f32[2,64,128]{2,1,0:T(8,128)S(1)}, f32[2,64,128]{2,1,0:T(8,128)S(1)}, u32[]{:S(2)}, u32[]{:S(2)}) collective-permute-start(f32[2,64,128]{2,1,0:T(8,128)S(1)} %shard_map.149.own_f), channel_id=1, source_target_pairs={{4,0},{8,4},{12,8},{5,1},{9,5},{13,9},{6,2},{10,6},{14,10},{7,3},{... | collective-permute-start | bytes 196616 | tf_op jit(solution)/shard_map/ppermute | solution.py:20
  33.0 3.0 %collective-permute-start = (f32[2,64,128]{2,1,0:T(8,128)S(1)}, f32[2,64,128]{2,1,0:T(8,128)S(1)}, u32[]{:S(2)}, u32[]{:S(2)}) collective-permute-start(f32[2,64,128]{2,1,0:T(8,128)S(1)} %shard_map.149.own_f), channel_id=1, source_target_pairs={{0,4},{4,8},{8,12},{1,5},{5,9},{9,13},{2,6},{6,10},{10,14},{3,7},{... | collective-permute-start | bytes 196616 | tf_op jit(solution)/shard_map/ppermute | solution.py:20
  36.6 0.0 collective-permute-done.1.next_f
  36.6 0.7 collective-permute-done.prev_f
  37.3 0.0 copy-done
  37.3 0.0 copy-start.3
  37.3 0.9 copy-done.3
  38.3 0.0 copy-start.4
  38.3 0.8 copy-done.4
  39.1 0.0 copy-start.7
  39.1 0.8 copy-done.7
  39.9 0.0 copy-start.11
  39.9 0.9 copy-done.11
  40.8 0.0 copy-start.5
  40.8 0.0 copy-start.6
  40.8 0.0 copy-start.9
  40.8 0.0 copy-start.10
  40.8 30.9 %shard_map.150 = (f32[3,128,128]{2,1,0:T(8,128)S(1)}, f32[128,128]{1,0:T(8,128)S(1)}) custom-call(f32[6,8192]{1,0:T(8,128)S(1)} %copy-done.3, f32[6,8192]{1,0:T(8,128)S(1)} %get-tuple-element.14.prev_q, f32[6,8192]{1,0:T(8,128)S(1)} %get-tuple-element.15.next_q, f32[2,64,128]{2,1,0:T(8,128)S(1)} %shard_map.149.own_f, ...), custom_call_target="tpu_custom_call" | custom-call | tf_op jit(solution)/shard_map/pallas_call | solution.py:441
  71.8 0.0 copy-done.1
  71.8 0.0 copy-done.5
  71.8 0.0 copy-done.6
  71.8 0.0 copy-done.9
  71.8 0.0 copy-done.10
  71.8 0.0 copy-start.8
  71.9 8.7 %shard_map.151 = (f32[6,8192]{1,0:T(8,128)S(1)}, f32[6,8192]{1,0:T(8,128)S(1)}) custom-call(s32[1]{0:T(128)S(6)} %copy.17.live_ref, f32[3,128,128]{2,1,0:T(8,128)S(1)} %get-tuple-element.17.delta_ref, f32[128,128]{1,0:T(8,128)S(1)} %get-tuple-element.18.eig_ref, s32[128,128]{1,0:T(8,128)S(1)} %bitcast.4, f32[6,16384]{1,0:T(8,128)S(1)} %copy-done, ...), custom_call_target="tpu_custom_call" | custom-call | tf_op jit(solution)/shard_map/pallas_call | solution.py:455
  80.6 1.9 %collective-permute-start.3 = (f32[6,8192]{1,0:T(8,128)S(1)}, f32[6,8192]{1,0:T(8,128)S(1)}, u32[]{:S(2)}, u32[]{:S(2)}) collective-permute-start(f32[6,8192]{1,0:T(8,128)S(1)} %get-tuple-element.19.own_q.disp_ref), channel_id=1, source_target_pairs={{4,0},{8,4},{12,8},{5,1},{9,5},{13,9},{6,2},{10,6},{14,10},{7,3},{... | collective-permute-start | bytes 589832 | tf_op jit(solution)/shard_map/ppermute | solution.py:20
  82.5 4.3 %collective-permute-start.2 = (f32[6,8192]{1,0:T(8,128)S(1)}, f32[6,8192]{1,0:T(8,128)S(1)}, u32[]{:S(2)}, u32[]{:S(2)}) collective-permute-start(f32[6,8192]{1,0:T(8,128)S(1)} %get-tuple-element.19.own_q.disp_ref), channel_id=1, source_target_pairs={{0,4},{4,8},{8,12},{1,5},{5,9},{9,13},{2,6},{6,10},{10,14},{3,7},{... | collective-permute-start | bytes 589832 | tf_op jit(solution)/shard_map/ppermute | solution.py:20
  86.8 2.1 %collective-permute-done.3.next_q = f32[6,8192]{1,0:T(8,128)S(1)} collective-permute-done((f32[6,8192]{1,0:T(8,128)S(1)}, f32[6,8192]{1,0:T(8,128)S(1)}, u32[]{:S(2)}, u32[]{:S(2)}) %collective-permute-start.3) | collective-permute-done | bytes 196640 | tf_op jit(solution)/shard_map/ppermute | solution.py:20
  88.9 1.2 collective-permute-done.2.prev_q
  90.1 0.0 copy-done.8
  90.1 26.0 %shard_map.152.delta_ref = f32[3,128,128]{2,1,0:T(8,128)S(1)} custom-call(f32[6,8192]{1,0:T(8,128)S(1)} %get-tuple-element.19.own_q.disp_ref, f32[6,8192]{1,0:T(8,128)S(1)} %collective-permute-done.2.prev_q, f32[6,8192]{1,0:T(8,128)S(1)} %collective-permute-done.3.next_q, s32[128,128]{1,0:T(8,128)S(1)} %bitcast.5, s32[128,128]{1,0:T(8,128)S(1)} %bitcast.8, ...), custom_call_target="tpu_custom_call" | custom-call | tf_op jit(solution)/shard_map/pallas_call | solution.py:451
  116.1 9.5 %shard_map.153 = (f32[6,8192]{1,0:T(8,128)}, f32[6,8192]{1,0:T(8,128)}) custom-call(s32[1]{0:T(128)S(6)} %copy.17.live_ref, f32[3,128,128]{2,1,0:T(8,128)S(1)} %shard_map.152.delta_ref, f32[128,128]{1,0:T(8,128)S(1)} %get-tuple-element.18.eig_ref, s32[128,128]{1,0:T(8,128)S(1)} %bitcast.6, f32[6,16384]{1,0:T(8,128)S(1)} %copy-done, ...), custom_call_target="tpu_custom_call" | custom-call | tf_op jit(solution)/shard_map/pallas_call | solution.py:455
  125.6 0.7 copy.18
Async XLA Ops:
  0.6 36.7 %copy-start = (f32[6,16384]{1,0:T(8,128)S(1)}, f32[6,16384]{1,0:T(8,128)}, u32[]{:S(2)}) copy-start(f32[6,16384]{1,0:T(8,128)} %arms_ref.7) | copy-start | bytes 1179652
  0.6 1.0 copy-start.2
  1.7 0.9 copy-start.12
  2.6 0.9 copy-start.13
  23.2 48.6 %copy-start.1 = (f32[9,16384]{1,0:T(8,128)S(1)}, f32[9,16384]{1,0:T(8,128)}, u32[]{:S(2)}) copy-start(f32[9,16384]{1,0:T(8,128)} %frame_ref.3) | copy-start | bytes 1769476
  23.2 0.8 copy-start.14
  30.4 6.2 %collective-permute-start.1 = (f32[2,64,128]{2,1,0:T(8,128)S(1)}, f32[2,64,128]{2,1,0:T(8,128)S(1)}, u32[]{:S(2)}, u32[]{:S(2)}) collective-permute-start(f32[2,64,128]{2,1,0:T(8,128)S(1)} %shard_map.149.own_f), channel_id=1, source_target_pairs={{4,0},{8,4},{12,8},{5,1},{9,5},{13,9},{6,2},{10,6},{14,10},{7,3},{... | collective-permute-start | bytes 196616 | tf_op jit(solution)/shard_map/ppermute | solution.py:20
  33.0 4.3 %collective-permute-start = (f32[2,64,128]{2,1,0:T(8,128)S(1)}, f32[2,64,128]{2,1,0:T(8,128)S(1)}, u32[]{:S(2)}, u32[]{:S(2)}) collective-permute-start(f32[2,64,128]{2,1,0:T(8,128)S(1)} %shard_map.149.own_f), channel_id=1, source_target_pairs={{0,4},{4,8},{8,12},{1,5},{5,9},{9,13},{2,6},{6,10},{10,14},{3,7},{... | collective-permute-start | bytes 196616 | tf_op jit(solution)/shard_map/ppermute | solution.py:20
  37.3 1.0 copy-start.3
  38.3 0.8 copy-start.4
  39.1 0.8 copy-start.7
  39.9 0.9 copy-start.11
  40.8 31.0 %copy-start.5 = (s32[16384]{0:T(1024)S(1)}, s32[16384]{0:T(1024)}, u32[]{:S(2)}) copy-start(s32[16384]{0:T(1024)} %param.19) | copy-start | bytes 196612
  40.8 31.0 %copy-start.6 = (f32[2,16384]{1,0:T(2,128)S(1)}, f32[2,16384]{1,0:T(2,128)}, u32[]{:S(2)}) copy-start(f32[2,16384]{1,0:T(2,128)} %stiff_ref.3) | copy-start | bytes 393220
  40.8 31.0 %copy-start.9 = (f32[2,8192]{1,0:T(2,128)S(1)}, f32[2,8192]{1,0:T(2,128)}, u32[]{:S(2)}) copy-start(f32[2,8192]{1,0:T(2,128)} %inertia_ref.3) | copy-start | bytes 196612
  40.8 31.0 %copy-start.10 = (f32[6,8192]{1,0:T(8,128)S(1)}, f32[6,8192]{1,0:T(8,128)}, u32[]{:S(2)}) copy-start(f32[6,8192]{1,0:T(8,128)} %vel_ref.1) | copy-start | bytes 589828
  71.8 18.3 %copy-start.8 = (s32[16384]{0:T(1024)S(1)}, s32[16384]{0:T(1024)}, u32[]{:S(2)}) copy-start(s32[16384]{0:T(1024)} %param.20) | copy-start | bytes 196612
  80.6 8.3 %collective-permute-start.3 = (f32[6,8192]{1,0:T(8,128)S(1)}, f32[6,8192]{1,0:T(8,128)S(1)}, u32[]{:S(2)}, u32[]{:S(2)}) collective-permute-start(f32[6,8192]{1,0:T(8,128)S(1)} %get-tuple-element.19.own_q.disp_ref), channel_id=1, source_target_pairs={{4,0},{8,4},{12,8},{5,1},{9,5},{13,9},{6,2},{10,6},{14,10},{7,3},{... | collective-permute-start | bytes 589832 | tf_op jit(solution)/shard_map/ppermute | solution.py:20
  82.5 7.6 %collective-permute-start.2 = (f32[6,8192]{1,0:T(8,128)S(1)}, f32[6,8192]{1,0:T(8,128)S(1)}, u32[]{:S(2)}, u32[]{:S(2)}) collective-permute-start(f32[6,8192]{1,0:T(8,128)S(1)} %get-tuple-element.19.own_q.disp_ref), channel_id=1, source_target_pairs={{0,4},{4,8},{8,12},{1,5},{5,9},{9,13},{2,6},{6,10},{10,14},{3,7},{... | collective-permute-start | bytes 589832 | tf_op jit(solution)/shard_map/ppermute | solution.py:20

commit v4 on v3

--- a/solution.py
+++ b/solution.py
@@ -148,7 +148,7 @@
     finish(disp_pair)
 
 
-WIDE = 256
+WIDE = 1024
 
 
 def stage_rows(staged, sources, first, total):

time: 127 us -> 107 us (0.84)
  Pallas kernels: 101 us -> 82 us
    pallas_call x1, Pallas kernels: 30.9 us -> 23 us  [body(): call(first_kernel, (shape(3, blocks, LANES), shape(blocks, LANES)), count...]
    pallas_call x1, Pallas kernels: 26 us -> 18.2 us  [body(): call(delta_kernel, jax.ShapeDtypeStruct((3, blocks, LANES), f32), count=6...]
    pallas_call x1, Pallas kernels: 6.32 us -> 2.8 us  [body(): call(host_kernel, jax.ShapeDtypeStruct((2, high, LANES), f32), count=2, s...]
where the time goes in v4:
time: 107 us
  Pallas kernels  82 us (77%)
  starting transfers between devices  11.7 us (11%)
  local copies, waits for them, and re-layouts  7.87 us (7%)
  waiting for transfers between devices  3.95 us (4%)
  between operations  1.45 us (1%)
    pallas_call x1, Pallas kernels, body(): call(first_kernel, (shape(3, blocks, LANES), shape(blocks, LANES)), count...  23 us
    pallas_call x1, Pallas kernels, body(): pl.pallas_call(flow_kernel, out_shape=(shape(*cell_start.shape), shape(ny...  19.8 us
    pallas_call x2, Pallas kernels, body(): call(update_kernel, (jax.ShapeDtypeStruct(disp.shape, f32), jax.ShapeDtyp...  18.3 us
    pallas_call x1, Pallas kernels, body(): call(delta_kernel, jax.ShapeDtypeStruct((3, blocks, LANES), f32), count=6...  18.2 us
    unnamed x31, local copies, waits for them, and re-layouts  7.87 us
    ppermute x2, starting transfers between devices, neighbours(): lax.ppermute(block, axis, forward)  7.22 us
    ppermute x2, starting transfers between devices, neighbours(): lax.ppermute(block, axis, backward)  4.52 us
    pallas_call x1, Pallas kernels, body(): call(host_kernel, jax.ShapeDtypeStruct((2, high, LANES), f32), count=2, s...  2.8 us
  transfers between devices with their start and end apart: 4, of which 3 were waited for; matrix products, arithmetic and copies ran while one was open for 0% of the time, Pallas kernels for 0%

profile of v4, /device:TPU:1, one launch (start us, length us, event | category | flops | bytes accessed | tf_op | source)
XLA Modules:
  0.0 107.1 jit_solution(12888514656134374081)
XLA Ops:
  0.6 0.0 copy-start
  0.6 0.0 copy-start.2
  0.7 1.0 copy-done.2
  1.7 0.0 copy-start.12
  1.7 0.9 copy-done.12
  2.6 0.0 copy-start.13
  2.6 0.9 copy-done.13
  3.5 19.8 %shard_map.148 = (f32[2,8,8,256]{3,2,1,0:T(8,128)S(1)}, f32[4,2,2,8,256]{4,3,2,1,0:T(8,128)S(1)}, f32[6,8192]{1,0:T(8,128)S(1)}, f32[6,8192]{1,0:T(8,128)S(1)}) custom-call(f32[2,8,8,256]{3,2,1,0:T(8,128)S(1)} %copy-done.12, f32[2,8,8,256]{3,2,1,0:T(8,128)S(1)} %copy-done.13, f32[6,8192]{1,0:T(8,128)S(1)} %copy-done.2), custom_call_target="tpu_custom_call" | custom-call | tf_op jit(solution)/shard_map/pallas_call | solution.py:413
  23.2 0.0 copy-start.1
  23.2 0.0 copy-start.14
  23.2 0.8 copy-done.14
  24.1 2.8 %shard_map.149.own_f = f32[2,64,128]{2,1,0:T(8,128)S(1)} custom-call(f32[4,2,2,8,256]{4,3,2,1,0:T(8,128)S(1)} %get-tuple-element.16.slab_ref, s32[64,128]{1,0:T(8,128)S(1)} %bitcast.9), custom_call_target="tpu_custom_call" | custom-call | tf_op jit(solution)/shard_map/pallas_call | solution.py:437
  26.9 2.6 %collective-permute-start.1 = (f32[2,64,128]{2,1,0:T(8,128)S(1)}, f32[2,64,128]{2,1,0:T(8,128)S(1)}, u32[]{:S(2)}, u32[]{:S(2)}) collective-permute-start(f32[2,64,128]{2,1,0:T(8,128)S(1)} %shard_map.149.own_f), channel_id=1, source_target_pairs={{4,0},{8,4},{12,8},{5,1},{9,5},{13,9},{6,2},{10,6},{14,10},{7,3},{... | collective-permute-start | bytes 196616 | tf_op jit(solution)/shard_map/ppermute | solution.py:20
  29.5 3.0 %collective-permute-start = (f32[2,64,128]{2,1,0:T(8,128)S(1)}, f32[2,64,128]{2,1,0:T(8,128)S(1)}, u32[]{:S(2)}, u32[]{:S(2)}) collective-permute-start(f32[2,64,128]{2,1,0:T(8,128)S(1)} %shard_map.149.own_f), channel_id=1, source_target_pairs={{0,4},{4,8},{8,12},{1,5},{5,9},{9,13},{2,6},{6,10},{10,14},{3,7},{... | collective-permute-start | bytes 196616 | tf_op jit(solution)/shard_map/ppermute | solution.py:20
  33.1 0.0 collective-permute-done.1.next_f
  33.1 0.7 collective-permute-done.prev_f
  33.8 0.0 copy-done
  33.8 0.0 copy-start.3
  33.8 0.9 copy-done.3
  34.7 0.0 copy-start.4
  34.7 0.8 copy-done.4
  35.6 0.0 copy-start.7
  35.6 0.8 copy-done.7
  36.4 0.0 copy-start.11
  36.4 0.9 copy-done.11
  37.3 0.0 copy-start.5
  37.3 0.0 copy-start.6
  37.3 0.0 copy-start.9
  37.3 0.0 copy-start.10
  37.3 23.0 %shard_map.150 = (f32[3,128,128]{2,1,0:T(8,128)S(1)}, f32[128,128]{1,0:T(8,128)S(1)}) custom-call(f32[6,8192]{1,0:T(8,128)S(1)} %copy-done.3, f32[6,8192]{1,0:T(8,128)S(1)} %get-tuple-element.14.prev_q, f32[6,8192]{1,0:T(8,128)S(1)} %get-tuple-element.15.next_q, f32[2,64,128]{2,1,0:T(8,128)S(1)} %shard_map.149.own_f, ...), custom_call_target="tpu_custom_call" | custom-call | tf_op jit(solution)/shard_map/pallas_call | solution.py:441
  60.3 0.0 copy-done.1
  60.4 0.0 copy-done.5
  60.4 0.0 copy-done.6
  60.4 0.0 copy-done.9
  60.4 0.0 copy-done.10
  60.4 0.0 copy-start.8
  60.4 8.7 %shard_map.151 = (f32[6,8192]{1,0:T(8,128)S(1)}, f32[6,8192]{1,0:T(8,128)S(1)}) custom-call(s32[1]{0:T(128)S(6)} %copy.17.live_ref, f32[3,128,128]{2,1,0:T(8,128)S(1)} %get-tuple-element.17.delta_ref, f32[128,128]{1,0:T(8,128)S(1)} %get-tuple-element.18.eig_ref, s32[128,128]{1,0:T(8,128)S(1)} %bitcast.4, f32[6,16384]{1,0:T(8,128)S(1)} %copy-done, ...), custom_call_target="tpu_custom_call" | custom-call | tf_op jit(solution)/shard_map/pallas_call | solution.py:455
  69.2 1.9 %collective-permute-start.3 = (f32[6,8192]{1,0:T(8,128)S(1)}, f32[6,8192]{1,0:T(8,128)S(1)}, u32[]{:S(2)}, u32[]{:S(2)}) collective-permute-start(f32[6,8192]{1,0:T(8,128)S(1)} %get-tuple-element.19.own_q.disp_ref), channel_id=1, source_target_pairs={{4,0},{8,4},{12,8},{5,1},{9,5},{13,9},{6,2},{10,6},{14,10},{7,3},{... | collective-permute-start | bytes 589832 | tf_op jit(solution)/shard_map/ppermute | solution.py:20
  71.1 4.3 %collective-permute-start.2 = (f32[6,8192]{1,0:T(8,128)S(1)}, f32[6,8192]{1,0:T(8,128)S(1)}, u32[]{:S(2)}, u32[]{:S(2)}) collective-permute-start(f32[6,8192]{1,0:T(8,128)S(1)} %get-tuple-element.19.own_q.disp_ref), channel_id=1, source_target_pairs={{0,4},{4,8},{8,12},{1,5},{5,9},{9,13},{2,6},{6,10},{10,14},{3,7},{... | collective-permute-start | bytes 589832 | tf_op jit(solution)/shard_map/ppermute | solution.py:20
  75.3 2.1 %collective-permute-done.3.next_q = f32[6,8192]{1,0:T(8,128)S(1)} collective-permute-done((f32[6,8192]{1,0:T(8,128)S(1)}, f32[6,8192]{1,0:T(8,128)S(1)}, u32[]{:S(2)}, u32[]{:S(2)}) %collective-permute-start.3) | collective-permute-done | bytes 196640 | tf_op jit(solution)/shard_map/ppermute | solution.py:20
  77.5 1.2 %collective-permute-done.2.prev_q = f32[6,8192]{1,0:T(8,128)S(1)} collective-permute-done((f32[6,8192]{1,0:T(8,128)S(1)}, f32[6,8192]{1,0:T(8,128)S(1)}, u32[]{:S(2)}, u32[]{:S(2)}) %collective-permute-start.2) | collective-permute-done | bytes 196640 | tf_op jit(solution)/shard_map/ppermute | solution.py:20
  78.6 0.0 copy-done.8
  78.6 18.2 %shard_map.152.delta_ref = f32[3,128,128]{2,1,0:T(8,128)S(1)} custom-call(f32[6,8192]{1,0:T(8,128)S(1)} %get-tuple-element.19.own_q.disp_ref, f32[6,8192]{1,0:T(8,128)S(1)} %collective-permute-done.2.prev_q, f32[6,8192]{1,0:T(8,128)S(1)} %collective-permute-done.3.next_q, s32[128,128]{1,0:T(8,128)S(1)} %bitcast.5, s32[128,128]{1,0:T(8,128)S(1)} %bitcast.8, ...), custom_call_target="tpu_custom_call" | custom-call | tf_op jit(solution)/shard_map/pallas_call | solution.py:451
  96.9 9.5 %shard_map.153 = (f32[6,8192]{1,0:T(8,128)}, f32[6,8192]{1,0:T(8,128)}) custom-call(s32[1]{0:T(128)S(6)} %copy.17.live_ref, f32[3,128,128]{2,1,0:T(8,128)S(1)} %shard_map.152.delta_ref, f32[128,128]{1,0:T(8,128)S(1)} %get-tuple-element.18.eig_ref, s32[128,128]{1,0:T(8,128)S(1)} %bitcast.6, f32[6,16384]{1,0:T(8,128)S(1)} %copy-done, ...), custom_call_target="tpu_custom_call" | custom-call | tf_op jit(solution)/shard_map/pallas_call | solution.py:455
  106.4 0.7 copy.18
Async XLA Ops:
  0.6 33.1 %copy-start = (f32[6,16384]{1,0:T(8,128)S(1)}, f32[6,16384]{1,0:T(8,128)}, u32[]{:S(2)}) copy-start(f32[6,16384]{1,0:T(8,128)} %arms_ref.7) | copy-start | bytes 1179652
  0.6 1.0 copy-start.2
  1.7 0.9 copy-start.12
  2.6 0.9 copy-start.13
  23.2 37.1 %copy-start.1 = (f32[9,16384]{1,0:T(8,128)S(1)}, f32[9,16384]{1,0:T(8,128)}, u32[]{:S(2)}) copy-start(f32[9,16384]{1,0:T(8,128)} %frame_ref.3) | copy-start | bytes 1769476
  23.2 0.8 copy-start.14
  26.9 6.2 %collective-permute-start.1 = (f32[2,64,128]{2,1,0:T(8,128)S(1)}, f32[2,64,128]{2,1,0:T(8,128)S(1)}, u32[]{:S(2)}, u32[]{:S(2)}) collective-permute-start(f32[2,64,128]{2,1,0:T(8,128)S(1)} %shard_map.149.own_f), channel_id=1, source_target_pairs={{4,0},{8,4},{12,8},{5,1},{9,5},{13,9},{6,2},{10,6},{14,10},{7,3},{... | collective-permute-start | bytes 196616 | tf_op jit(solution)/shard_map/ppermute | solution.py:20
  29.5 4.3 %collective-permute-start = (f32[2,64,128]{2,1,0:T(8,128)S(1)}, f32[2,64,128]{2,1,0:T(8,128)S(1)}, u32[]{:S(2)}, u32[]{:S(2)}) collective-permute-start(f32[2,64,128]{2,1,0:T(8,128)S(1)} %shard_map.149.own_f), channel_id=1, source_target_pairs={{0,4},{4,8},{8,12},{1,5},{5,9},{9,13},{2,6},{6,10},{10,14},{3,7},{... | collective-permute-start | bytes 196616 | tf_op jit(solution)/shard_map/ppermute | solution.py:20
  33.8 1.0 copy-start.3
  34.7 0.8 copy-start.4
  35.6 0.8 copy-start.7
  36.4 0.9 copy-start.11
  37.3 23.0 %copy-start.5 = (s32[16384]{0:T(1024)S(1)}, s32[16384]{0:T(1024)}, u32[]{:S(2)}) copy-start(s32[16384]{0:T(1024)} %param.19) | copy-start | bytes 196612
  37.3 23.1 %copy-start.6 = (f32[2,16384]{1,0:T(2,128)S(1)}, f32[2,16384]{1,0:T(2,128)}, u32[]{:S(2)}) copy-start(f32[2,16384]{1,0:T(2,128)} %stiff_ref.3) | copy-start | bytes 393220
  37.3 23.1 %copy-start.9 = (f32[2,8192]{1,0:T(2,128)S(1)}, f32[2,8192]{1,0:T(2,128)}, u32[]{:S(2)}) copy-start(f32[2,8192]{1,0:T(2,128)} %inertia_ref.3) | copy-start | bytes 196612
  37.3 23.1 %copy-start.10 = (f32[6,8192]{1,0:T(8,128)S(1)}, f32[6,8192]{1,0:T(8,128)}, u32[]{:S(2)}) copy-start(f32[6,8192]{1,0:T(8,128)} %vel_ref.1) | copy-start | bytes 589828
  60.4 18.2 %copy-start.8 = (s32[16384]{0:T(1024)S(1)}, s32[16384]{0:T(1024)}, u32[]{:S(2)}) copy-start(s32[16384]{0:T(1024)} %param.20) | copy-start | bytes 196612
  69.2 8.3 %collective-permute-start.3 = (f32[6,8192]{1,0:T(8,128)S(1)}, f32[6,8192]{1,0:T(8,128)S(1)}, u32[]{:S(2)}, u32[]{:S(2)}) collective-permute-start(f32[6,8192]{1,0:T(8,128)S(1)} %get-tuple-element.19.own_q.disp_ref), channel_id=1, source_target_pairs={{4,0},{8,4},{12,8},{5,1},{9,5},{13,9},{6,2},{10,6},{14,10},{7,3},{... | collective-permute-start | bytes 589832 | tf_op jit(solution)/shard_map/ppermute | solution.py:20
  71.1 7.6 %collective-permute-start.2 = (f32[6,8192]{1,0:T(8,128)S(1)}, f32[6,8192]{1,0:T(8,128)S(1)}, u32[]{:S(2)}, u32[]{:S(2)}) collective-permute-start(f32[6,8192]{1,0:T(8,128)S(1)} %get-tuple-element.19.own_q.disp_ref), channel_id=1, source_target_pairs={{0,4},{4,8},{8,12},{1,5},{5,9},{9,13},{2,6},{6,10},{10,14},{3,7},{... | collective-permute-start | bytes 589832 | tf_op jit(solution)/shard_map/ppermute | solution.py:20
